TPU v7x, 32 devices: a whole 2x2x4 slice. The times are simulated.
32 devices in a mesh: chan: 8 (over z, x), tm: 4 (over y, core).
Axes of the slice: x: 2, y: 2, z: 4, core: 2. Of those that a mesh axis runs over, the one named last changes fastest.
Arguments:
- waveform: bfloat16 [1024, 49152], P('chan', 'tm'), may hold values from -6 to 6
- coords: int32 [2, 1024], replicated, may hold values from 0 to 9999
- directions: int32 [2, 2048], replicated, may hold values from -32 to 32
- bins: int32 [96], replicated, may hold values from 1 to 511
Outputs:
- beams: float32 [96, 2, 96, 2048], P('chan', None, 'tm')
All inputs are finite; a program needn't handle non-finite values.
Results may differ from a plain program's by a relative error of at most 0.0045.
Values may be sent and summed in bfloat16 or wider, within the bound.
A program may use at most 128 MiB of HBM per device.

v0:
```python
import math

import jax
import jax.numpy as jnp
from jax import lax
from jax.sharding import PartitionSpec as P

FL = 1024


phase_steps = 1048576


def from_behind(value, axis, by):
    count = lax.axis_size(axis)
    pairs = [(i, i + by) for i in range(count) if 0 <= i + by < count]
    return lax.ppermute(value, axis, pairs)


def dft_table(bins, frame_length):
    sample_index = jnp.arange(frame_length, dtype=jnp.int32)
    product = jnp.mod(sample_index[:, None] * bins[None, :], frame_length)
    angle = product.astype(jnp.float32) * jnp.float32(2.0 * math.pi / frame_length)
    window = 0.5 - 0.5 * jnp.cos(
        sample_index.astype(jnp.float32) * jnp.float32(2.0 * math.pi / frame_length)
    )
    norm_factor = jnp.float32(1.0 / math.sqrt(frame_length))
    real_cols = window[:, None] * jnp.cos(angle) * norm_factor
    imag_cols = -window[:, None] * jnp.sin(angle) * norm_factor
    return jnp.concatenate([real_cols, imag_cols], axis=1).astype(jnp.bfloat16)


def group_beams(bin_group, real_group, imag_group, offsets):
    left_top = jnp.concatenate([real_group, -imag_group], axis=2)
    left_low = jnp.concatenate([imag_group, real_group], axis=2)
    stacked_left = jnp.concatenate([left_top, left_low], axis=1)
    reduced = jnp.mod(offsets, phase_steps)
    turns = jnp.mod(bin_group[:, None, None] * reduced[None, :, :], phase_steps)
    angle = turns.astype(jnp.float32) * jnp.float32(2.0 * math.pi / phase_steps)
    steering = jnp.concatenate([jnp.cos(angle), jnp.sin(angle)], axis=1).astype(jnp.bfloat16)
    return jnp.einsum("kfc,kcb->kfb", stacked_left, steering, preferred_element_type=jnp.float32)


def group_size():
    best = 1
    for candidate in range(1, 5):
        best = candidate
    return best


def channel_offsets(own_coords, directions):
    return (
        own_coords[0][:, None] * directions[0][None, :]
        + own_coords[1][:, None] * directions[1][None, :]
    )


def on_device(waveform, coords, directions, bins):
    channels_dev = waveform.shape[0]
    hop_length = FL // 2
    frames_dev = waveform.shape[1] // hop_length
    bin_count = bins.shape[0]
    beam_count = directions.shape[1]
    chan_count = lax.axis_size("chan")
    own_bins = bin_count // chan_count
    leading = waveform[:, :hop_length]
    following = from_behind(leading, "tm", -1)
    halves = jnp.concatenate([waveform, following], axis=1).reshape(
        channels_dev, frames_dev + 1, hop_length
    )
    transform = dft_table(bins, FL)
    front_half = halves[:, :-1].reshape(-1, hop_length)
    back_half = halves[:, 1:].reshape(-1, hop_length)
    spectra = jnp.dot(
        front_half, transform[:hop_length], preferred_element_type=jnp.float32
    ) + jnp.dot(back_half, transform[hop_length:], preferred_element_type=jnp.float32)
    spectra = spectra.astype(jnp.bfloat16).reshape(channels_dev, frames_dev, 2 * bin_count)
    stacked = jnp.transpose(spectra, (2, 1, 0)).reshape(2, bin_count, frames_dev, channels_dev)
    norm_factor = jnp.float32(1.0 / math.sqrt(channels_dev * chan_count))
    own_coords = lax.dynamic_slice_in_dim(
        coords, lax.axis_index("chan") * channels_dev, channels_dev, 1
    )
    offsets = channel_offsets(own_coords, directions)
    width = group_size()
    group_count = lax.axis_size("chan") * own_bins // width
    bin_slice = bins.reshape(group_count, width)
    real_rows = stacked[0].reshape(group_count, width, frames_dev, channels_dev)
    imag_rows = stacked[1].reshape(group_count, width, frames_dev, channels_dev)

    def single(member):
        bin_group, real_group, imag_group = member
        return group_beams(bin_group, real_group, imag_group, offsets)

    result = lax.map(single, (bin_slice, real_rows, imag_rows))
    summed = lax.psum_scatter(
        result.reshape(lax.axis_size("chan") * own_bins, 2 * frames_dev, beam_count),
        "chan",
        scatter_dimension=0,
        tiled=True,
    )
    summed = summed * norm_factor
    return summed.reshape(own_bins, 2, frames_dev, beam_count)


def solution(mesh):
    return jax.shard_map(
        on_device,
        mesh=mesh,
        in_specs=(P("chan", "tm"), P(), P(), P()),
        out_specs=P("chan", None, "tm", None),
        check_vma=False,
    )
```

profile of v0, /device:TPU:0, one launch (start us, length us, event | category | flops | bytes accessed | tf_op | source)
XLA Modules:
  0.0 1124.9 jit_solution(2376146629118253737)
XLA Ops:
  6.5 3.5 copy.13
  12.2 3.1 multiply_convert_fusion
  17.5 4.1 fusion.42
  21.6 3.8 copy.14
  25.4 4.9 copy.15
  36.3 466.6 %while.15 = (s32[]{:T(128)}, f32[24,4,48,2048]{3,2,1,0:T(8,128)}, bf16[24,4,24,128]{3,2,1,0:T(8,128)(2,1)S(1)}, bf16[24,4,24,128]{3,2,1,0:T(8,128)(2,1)S(1)}, s3...) while((s32[]{:T(128)}, f32[24,4,48,2048]{3,2,1,0:T(8,128)}, ...), condition=%wide.region_1.2_spmd.clone.clone, body=%wide.region_0.1_spmd.clone.clone.sunk | while | flops 230567936 | bytes 12273313 | solution.py:94
  37.1 16.8 %cosine_convert_fusion.2 = (bf16[4,128,2048]{2,1,0:T(8,128)(2,1)S(1)}, bf16[4,128,2048]{2,1,0:T(8,128)(2,1)S(1)}) fusion(s32[128,2048]{1,0:T(8,128)S(1)} %add_select_fusion.4, s32[4]{0:T(128)S(1)} %fusion.54), kind=kLoop, calls=%fused_computation.15.clone.1 | loop fusion | flops 16777216 | bytes 5242896 | tf_op jit(solution)/shard_map/convert
  56.5 16.8 %cosine_convert_fusion.2 = (bf16[4,128,2048]{2,1,0:T(8,128)(2,1)S(1)}, bf16[4,128,2048]{2,1,0:T(8,128)(2,1)S(1)}) fusion(s32[128,2048]{1,0:T(8,128)S(1)} %add_select_fusion.4, s32[4]{0:T(128)S(1)} %fusion.54), kind=kLoop, calls=%fused_computation.15.clone.1 | loop fusion | flops 16777216 | bytes 5242896 | tf_op jit(solution)/shard_map/convert
  76.0 16.8 %cosine_convert_fusion.2 = (bf16[4,128,2048]{2,1,0:T(8,128)(2,1)S(1)}, bf16[4,128,2048]{2,1,0:T(8,128)(2,1)S(1)}) fusion(s32[128,2048]{1,0:T(8,128)S(1)} %add_select_fusion.4, s32[4]{0:T(128)S(1)} %fusion.54), kind=kLoop, calls=%fused_computation.15.clone.1 | loop fusion | flops 16777216 | bytes 5242896 | tf_op jit(solution)/shard_map/convert
  95.4 16.8 %cosine_convert_fusion.2 = (bf16[4,128,2048]{2,1,0:T(8,128)(2,1)S(1)}, bf16[4,128,2048]{2,1,0:T(8,128)(2,1)S(1)}) fusion(s32[128,2048]{1,0:T(8,128)S(1)} %add_select_fusion.4, s32[4]{0:T(128)S(1)} %fusion.54), kind=kLoop, calls=%fused_computation.15.clone.1 | loop fusion | flops 16777216 | bytes 5242896 | tf_op jit(solution)/shard_map/convert
  114.8 16.8 %cosine_convert_fusion.2 = (bf16[4,128,2048]{2,1,0:T(8,128)(2,1)S(1)}, bf16[4,128,2048]{2,1,0:T(8,128)(2,1)S(1)}) fusion(s32[128,2048]{1,0:T(8,128)S(1)} %add_select_fusion.4, s32[4]{0:T(128)S(1)} %fusion.54), kind=kLoop, calls=%fused_computation.15.clone.1 | loop fusion | flops 16777216 | bytes 5242896 | tf_op jit(solution)/shard_map/convert
  134.3 16.8 %cosine_convert_fusion.2 = (bf16[4,128,2048]{2,1,0:T(8,128)(2,1)S(1)}, bf16[4,128,2048]{2,1,0:T(8,128)(2,1)S(1)}) fusion(s32[128,2048]{1,0:T(8,128)S(1)} %add_select_fusion.4, s32[4]{0:T(128)S(1)} %fusion.54), kind=kLoop, calls=%fused_computation.15.clone.1 | loop fusion | flops 16777216 | bytes 5242896 | tf_op jit(solution)/shard_map/convert
  153.8 16.8 %cosine_convert_fusion.2 = (bf16[4,128,2048]{2,1,0:T(8,128)(2,1)S(1)}, bf16[4,128,2048]{2,1,0:T(8,128)(2,1)S(1)}) fusion(s32[128,2048]{1,0:T(8,128)S(1)} %add_select_fusion.4, s32[4]{0:T(128)S(1)} %fusion.54), kind=kLoop, calls=%fused_computation.15.clone.1 | loop fusion | flops 16777216 | bytes 5242896 | tf_op jit(solution)/shard_map/convert
  173.2 16.8 %cosine_convert_fusion.2 = (bf16[4,128,2048]{2,1,0:T(8,128)(2,1)S(1)}, bf16[4,128,2048]{2,1,0:T(8,128)(2,1)S(1)}) fusion(s32[128,2048]{1,0:T(8,128)S(1)} %add_select_fusion.4, s32[4]{0:T(128)S(1)} %fusion.54), kind=kLoop, calls=%fused_computation.15.clone.1 | loop fusion | flops 16777216 | bytes 5242896 | tf_op jit(solution)/shard_map/convert
  192.6 16.8 %cosine_convert_fusion.2 = (bf16[4,128,2048]{2,1,0:T(8,128)(2,1)S(1)}, bf16[4,128,2048]{2,1,0:T(8,128)(2,1)S(1)}) fusion(s32[128,2048]{1,0:T(8,128)S(1)} %add_select_fusion.4, s32[4]{0:T(128)S(1)} %fusion.54), kind=kLoop, calls=%fused_computation.15.clone.1 | loop fusion | flops 16777216 | bytes 5242896 | tf_op jit(solution)/shard_map/convert
  212.0 16.8 %cosine_convert_fusion.2 = (bf16[4,128,2048]{2,1,0:T(8,128)(2,1)S(1)}, bf16[4,128,2048]{2,1,0:T(8,128)(2,1)S(1)}) fusion(s32[128,2048]{1,0:T(8,128)S(1)} %add_select_fusion.4, s32[4]{0:T(128)S(1)} %fusion.54), kind=kLoop, calls=%fused_computation.15.clone.1 | loop fusion | flops 16777216 | bytes 5242896 | tf_op jit(solution)/shard_map/convert
  231.5 16.8 %cosine_convert_fusion.2 = (bf16[4,128,2048]{2,1,0:T(8,128)(2,1)S(1)}, bf16[4,128,2048]{2,1,0:T(8,128)(2,1)S(1)}) fusion(s32[128,2048]{1,0:T(8,128)S(1)} %add_select_fusion.4, s32[4]{0:T(128)S(1)} %fusion.54), kind=kLoop, calls=%fused_computation.15.clone.1 | loop fusion | flops 16777216 | bytes 5242896 | tf_op jit(solution)/shard_map/convert
  250.9 16.8 %cosine_convert_fusion.2 = (bf16[4,128,2048]{2,1,0:T(8,128)(2,1)S(1)}, bf16[4,128,2048]{2,1,0:T(8,128)(2,1)S(1)}) fusion(s32[128,2048]{1,0:T(8,128)S(1)} %add_select_fusion.4, s32[4]{0:T(128)S(1)} %fusion.54), kind=kLoop, calls=%fused_computation.15.clone.1 | loop fusion | flops 16777216 | bytes 5242896 | tf_op jit(solution)/shard_map/convert
  270.3 16.8 %cosine_convert_fusion.2 = (bf16[4,128,2048]{2,1,0:T(8,128)(2,1)S(1)}, bf16[4,128,2048]{2,1,0:T(8,128)(2,1)S(1)}) fusion(s32[128,2048]{1,0:T(8,128)S(1)} %add_select_fusion.4, s32[4]{0:T(128)S(1)} %fusion.54), kind=kLoop, calls=%fused_computation.15.clone.1 | loop fusion | flops 16777216 | bytes 5242896 | tf_op jit(solution)/shard_map/convert
  289.7 16.8 %cosine_convert_fusion.2 = (bf16[4,128,2048]{2,1,0:T(8,128)(2,1)S(1)}, bf16[4,128,2048]{2,1,0:T(8,128)(2,1)S(1)}) fusion(s32[128,2048]{1,0:T(8,128)S(1)} %add_select_fusion.4, s32[4]{0:T(128)S(1)} %fusion.54), kind=kLoop, calls=%fused_computation.15.clone.1 | loop fusion | flops 16777216 | bytes 5242896 | tf_op jit(solution)/shard_map/convert
  309.1 16.8 %cosine_convert_fusion.2 = (bf16[4,128,2048]{2,1,0:T(8,128)(2,1)S(1)}, bf16[4,128,2048]{2,1,0:T(8,128)(2,1)S(1)}) fusion(s32[128,2048]{1,0:T(8,128)S(1)} %add_select_fusion.4, s32[4]{0:T(128)S(1)} %fusion.54), kind=kLoop, calls=%fused_computation.15.clone.1 | loop fusion | flops 16777216 | bytes 5242896 | tf_op jit(solution)/shard_map/convert
  328.6 16.8 %cosine_convert_fusion.2 = (bf16[4,128,2048]{2,1,0:T(8,128)(2,1)S(1)}, bf16[4,128,2048]{2,1,0:T(8,128)(2,1)S(1)}) fusion(s32[128,2048]{1,0:T(8,128)S(1)} %add_select_fusion.4, s32[4]{0:T(128)S(1)} %fusion.54), kind=kLoop, calls=%fused_computation.15.clone.1 | loop fusion | flops 16777216 | bytes 5242896 | tf_op jit(solution)/shard_map/convert
  348.0 16.8 %cosine_convert_fusion.2 = (bf16[4,128,2048]{2,1,0:T(8,128)(2,1)S(1)}, bf16[4,128,2048]{2,1,0:T(8,128)(2,1)S(1)}) fusion(s32[128,2048]{1,0:T(8,128)S(1)} %add_select_fusion.4, s32[4]{0:T(128)S(1)} %fusion.54), kind=kLoop, calls=%fused_computation.15.clone.1 | loop fusion | flops 16777216 | bytes 5242896 | tf_op jit(solution)/shard_map/convert
  367.5 16.8 %cosine_convert_fusion.2 = (bf16[4,128,2048]{2,1,0:T(8,128)(2,1)S(1)}, bf16[4,128,2048]{2,1,0:T(8,128)(2,1)S(1)}) fusion(s32[128,2048]{1,0:T(8,128)S(1)} %add_select_fusion.4, s32[4]{0:T(128)S(1)} %fusion.54), kind=kLoop, calls=%fused_computation.15.clone.1 | loop fusion | flops 16777216 | bytes 5242896 | tf_op jit(solution)/shard_map/convert
  386.9 16.8 %cosine_convert_fusion.2 = (bf16[4,128,2048]{2,1,0:T(8,128)(2,1)S(1)}, bf16[4,128,2048]{2,1,0:T(8,128)(2,1)S(1)}) fusion(s32[128,2048]{1,0:T(8,128)S(1)} %add_select_fusion.4, s32[4]{0:T(128)S(1)} %fusion.54), kind=kLoop, calls=%fused_computation.15.clone.1 | loop fusion | flops 16777216 | bytes 5242896 | tf_op jit(solution)/shard_map/convert
  406.4 16.8 %cosine_convert_fusion.2 = (bf16[4,128,2048]{2,1,0:T(8,128)(2,1)S(1)}, bf16[4,128,2048]{2,1,0:T(8,128)(2,1)S(1)}) fusion(s32[128,2048]{1,0:T(8,128)S(1)} %add_select_fusion.4, s32[4]{0:T(128)S(1)} %fusion.54), kind=kLoop, calls=%fused_computation.15.clone.1 | loop fusion | flops 16777216 | bytes 5242896 | tf_op jit(solution)/shard_map/convert
  425.8 16.8 %cosine_convert_fusion.2 = (bf16[4,128,2048]{2,1,0:T(8,128)(2,1)S(1)}, bf16[4,128,2048]{2,1,0:T(8,128)(2,1)S(1)}) fusion(s32[128,2048]{1,0:T(8,128)S(1)} %add_select_fusion.4, s32[4]{0:T(128)S(1)} %fusion.54), kind=kLoop, calls=%fused_computation.15.clone.1 | loop fusion | flops 16777216 | bytes 5242896 | tf_op jit(solution)/shard_map/convert
  445.3 16.8 %cosine_convert_fusion.2 = (bf16[4,128,2048]{2,1,0:T(8,128)(2,1)S(1)}, bf16[4,128,2048]{2,1,0:T(8,128)(2,1)S(1)}) fusion(s32[128,2048]{1,0:T(8,128)S(1)} %add_select_fusion.4, s32[4]{0:T(128)S(1)} %fusion.54), kind=kLoop, calls=%fused_computation.15.clone.1 | loop fusion | flops 16777216 | bytes 5242896 | tf_op jit(solution)/shard_map/convert
  464.7 16.8 %cosine_convert_fusion.2 = (bf16[4,128,2048]{2,1,0:T(8,128)(2,1)S(1)}, bf16[4,128,2048]{2,1,0:T(8,128)(2,1)S(1)}) fusion(s32[128,2048]{1,0:T(8,128)S(1)} %add_select_fusion.4, s32[4]{0:T(128)S(1)} %fusion.54), kind=kLoop, calls=%fused_computation.15.clone.1 | loop fusion | flops 16777216 | bytes 5242896 | tf_op jit(solution)/shard_map/convert
  484.1 16.8 %cosine_convert_fusion.2 = (bf16[4,128,2048]{2,1,0:T(8,128)(2,1)S(1)}, bf16[4,128,2048]{2,1,0:T(8,128)(2,1)S(1)}) fusion(s32[128,2048]{1,0:T(8,128)S(1)} %add_select_fusion.4, s32[4]{0:T(128)S(1)} %fusion.54), kind=kLoop, calls=%fused_computation.15.clone.1 | loop fusion | flops 16777216 | bytes 5242896 | tf_op jit(solution)/shard_map/convert
  503.0 609.8 %reduce-scatter.2.cloned.1.call-done = f32[12,48,2048]{2,1,0:T(8,128)} async-done(((f32[96,48,2048]{2,1,0:T(8,128)}), f32[12,48,2048]{2,1,0:T(8,128)}) %reduce-scatter.2.cloned.1.call-update) | async-done | bytes 4718608 | tf_op jit(solution)/shard_map/reduce_scatter | solution.py:95
  1112.8 5.2 broadcast_multiply_fusion
  (150 shorter events, 73.0 us)
Async XLA Ops:
  6.5 8.7 copy-start
  6.5 5.5 copy-start.4
  6.5 5.6 copy-start.5
  6.5 1106.2 %reduce-scatter.2.cloned.1.call-start = ((), (), s32[]{:S(2)}) async-start(), calls=%async_computation.1 | async-start | bytes 42467328 | tf_op jit(solution)/shard_map/reduce_scatter | solution.py:95
  10.7 4.6 collective-permute-start
  30.3 2.3 copy-start.2
  30.4 2.3 copy-start.3
  503.0 615.0 %copy-start.1 = (s32[2,1024]{1,0:T(2,128)S(1)}, s32[2,1024]{1,0:T(2,128)}, u32[]{:S(2)}) copy-start(s32[2,1024]{1,0:T(2,128)} %param.7) | copy-start | bytes 24580
Sparse Core Ops, SparseCore 0:
  503.1 609.6 reduce-scatter.1
where the time goes:
time: 1130 us; the launch traced here: 1120 us
  waiting for transfers between devices  610 us (54%)
  other arithmetic  427 us (38%)
  matrix products  52.1 us (5%)
  local copies, waits for them, and re-layouts  20 us (2%)
  between operations  13.5 us (1%)
    reduce_scatter x1, waiting for transfers between devices, on_device(): lax.psum_scatter(result.reshape(lax.axis_size('chan') * own_bins, 2 * fra...  610 us
    another operation x25, other arithmetic  406 us
    dot_general x24, matrix products, group_beams(): jnp.einsum('kfc,kcb->kfb', stacked_left, steering, preferred_element_type...  48.5 us
  transfers between devices with their start and end apart: 2, of which 1 were waited for; matrix products, arithmetic and copies ran while one was open for 0% of the time, Pallas kernels for 0%

commit v1 on v0

v1 whole, which is shorter than its diff:
```python
import functools
import math

import jax
import jax.numpy as jnp
import numpy as np
from jax import lax
from jax.experimental import pallas as pl
from jax.experimental.pallas import tpu as pltpu
from jax.sharding import PartitionSpec as P

FL = 1024
PHASE_STEPS = 1048576
LANES = 128
BEAM_TILE = 512


def half_angle_fit():
    r = 0.5 * np.cos(np.pi * (np.arange(2000) + 0.5) / 4000)
    w = r * r
    sine = np.polynomial.polynomial.polyfit(w, np.sqrt(2) * np.sin(np.pi * r) / r, 2)
    cosine = np.polynomial.polynomial.polyfit(w, np.sqrt(2) * np.cos(np.pi * r), 3)
    return [float(c) for c in sine], [float(c) for c in cosine]


def dft_table(bins, frame_length):
    sample_index = jnp.arange(frame_length, dtype=jnp.int32)
    product = jnp.mod(bins[:, None] * sample_index[None, :], frame_length)
    angle = product.astype(jnp.float32) * jnp.float32(2.0 * math.pi / frame_length)
    window = 0.5 - 0.5 * jnp.cos(
        sample_index.astype(jnp.float32) * jnp.float32(2.0 * math.pi / frame_length)
    )
    scaled = window[None, :]
    norm_factor = jnp.float32(1.0 / math.sqrt(frame_length))
    real_rows = scaled * jnp.cos(angle) * norm_factor
    imag_rows = -scaled * jnp.sin(angle) * norm_factor
    return jnp.concatenate([real_rows, imag_rows], axis=0).astype(jnp.bfloat16)


def spectra_kernel(table_ref, wave_ref, next_ref, out_ref, rows_ref):
    hop = FL // 2
    frames = wave_ref.shape[1] // hop
    bin_count = table_ref.shape[0] // 2
    for t in range(frames):
        if t < frames - 1:
            frame = wave_ref[:, t * hop : t * hop + FL]
        else:
            frame = jnp.concatenate([wave_ref[:, t * hop :], next_ref[...]], axis=1)
        part = lax.dot_general(
            table_ref[...], frame, (((1,), (1,)), ((), ())), preferred_element_type=jnp.float32
        )
        rows_ref[:, t, :] = part[:bin_count]
        rows_ref[:, frames + t, :] = part[bin_count:]
    out_ref[...] = rows_ref[...].astype(jnp.bfloat16)


def spectra_rows(table, waveform, following):
    channels, samples = waveform.shape
    frames = samples // (FL // 2)
    bin_count = table.shape[0] // 2
    return pl.pallas_call(
        spectra_kernel,
        out_shape=jax.ShapeDtypeStruct((bin_count, 2 * frames, channels), jnp.bfloat16),
        scratch_shapes=[pltpu.VMEM((bin_count, 2 * frames, channels), jnp.float32)],
        compiler_params=pltpu.CompilerParams(vmem_limit_bytes=32 * 2**20),
    )(table, waveform, following)


def beam_kernel(bins_ref, coords_ref, directions_ref, x_ref, out_ref, offsets_ref, cos_ref, sin_ref, *, scale):
    sine, cosine = half_angle_fit()
    sources, _, rows, width = x_ref.shape
    channels = sources * width
    step = 16

    @pl.when(pl.program_id(1) == 0)
    def _():
        @pl.loop(0, channels, step=step)
        def _(at):
            piece = pl.ds(at, step)
            offsets_ref[piece, :] = (
                coords_ref[piece, 0:1] * directions_ref[0:1, :] + coords_ref[piece, 1:2] * directions_ref[1:2, :]
            )

    turn = bins_ref[pl.program_id(1)] * (2**32 // PHASE_STEPS)
    frames = rows // 2
    by_cos = jnp.zeros((rows, out_ref.shape[2]), jnp.float32)
    by_sin = jnp.zeros((rows, out_ref.shape[2]), jnp.float32)
    group = 2
    for first in range(0, sources, group):
        for at in range(first * width, (first + group) * width, step):
            x = (offsets_ref[at : at + step, :] * turn).astype(jnp.float32) * 2.0**-32
            w = x * x
            s = ((sine[2] * w + sine[1]) * w + sine[0]) * x
            c = ((cosine[3] * w + cosine[2]) * w + cosine[1]) * w + cosine[0]
            cos_ref[at : at + step, :] = (1.0 - s * s).astype(jnp.bfloat16)
            sin_ref[at : at + step, :] = (s * c).astype(jnp.bfloat16)
        left = jnp.concatenate([x_ref[first + k, 0] for k in range(group)], axis=1)
        rows_of = slice(first * width, (first + group) * width)
        by_cos += jnp.dot(left, cos_ref[rows_of, :], preferred_element_type=jnp.float32)
        by_sin += jnp.dot(left, sin_ref[rows_of, :], preferred_element_type=jnp.float32)
    out_ref[0, :frames, :] = (by_cos[:frames] - by_sin[frames:]) * scale
    out_ref[0, frames:, :] = (by_cos[frames:] + by_sin[:frames]) * scale


def form_beams(own_bins, coords, directions, received):
    sources, bins_dev, rows, width = received.shape
    channels = sources * width
    beams = directions.shape[1]
    tile = min(BEAM_TILE, beams)
    scale = 1.0 / math.sqrt(channels)
    return pl.pallas_call(
        functools.partial(beam_kernel, scale=scale),
        out_shape=jax.ShapeDtypeStruct((bins_dev, rows, beams), jnp.float32),
        grid_spec=pltpu.PrefetchScalarGridSpec(
            num_scalar_prefetch=1,
            grid=(beams // tile, bins_dev),
            in_specs=[
                pl.BlockSpec((channels, 2), lambda j, f, s: (0, 0)),
                pl.BlockSpec((2, tile), lambda j, f, s: (0, j)),
                pl.BlockSpec((sources, 1, rows, width), lambda j, f, s: (0, f, 0, 0)),
            ],
            out_specs=pl.BlockSpec((1, rows, tile), lambda j, f, s: (f, 0, j)),
            scratch_shapes=[
                pltpu.VMEM((channels, tile), jnp.int32),
                pltpu.VMEM((channels, tile), jnp.bfloat16),
                pltpu.VMEM((channels, tile), jnp.bfloat16),
            ],
        ),
        compiler_params=pltpu.CompilerParams(vmem_limit_bytes=48 * 2**20),
    )(own_bins, coords.T, directions, received)


def on_device(waveform, coords, directions, bins):
    channels_dev = waveform.shape[0]
    hop_length = FL // 2
    frames_dev = waveform.shape[1] // hop_length
    chan_count = lax.axis_size("chan")
    tm_count = lax.axis_size("tm")
    bins_dev = bins.shape[0] // chan_count
    following = lax.ppermute(
        waveform[:, :hop_length], "tm", [(i, i - 1) for i in range(1, tm_count)]
    )
    table = dft_table(bins, FL)
    rows = spectra_rows(table, waveform, following)
    rows = rows.reshape(chan_count, bins_dev, 2 * frames_dev, channels_dev)
    received = lax.all_to_all(rows, "chan", 0, 0)
    own_bins = lax.dynamic_slice_in_dim(bins, lax.axis_index("chan") * bins_dev, bins_dev, 0)
    beams = form_beams(own_bins, coords, directions, received)
    return beams.reshape(bins_dev, 2, frames_dev, directions.shape[1])


def solution(mesh):
    return jax.shard_map(
        on_device,
        mesh=mesh,
        in_specs=(P("chan", "tm"), P(), P(), P()),
        out_specs=P("chan", None, "tm", None),
        check_vma=False,
    )
```

time: 1130 us -> 142 us (0.13)
  waiting for transfers between devices: 610 us -> 29.2 us
  other arithmetic: 427 us -> 2.63 us
  Pallas kernels: 0 us -> 97.6 us
  matrix products: 52.1 us -> 0 us
  local copies, waits for them, and re-layouts: 20 us -> 3.1 us
  between operations: 13.5 us -> 0.06 us
    reduce_scatter x1 -> x0, waiting for transfers between devices: 610 us -> none  [on_device(): lax.psum_scatter(result.reshape(lax.axis_size('chan') * own_bins, 2 * fra...]
    another operation x25 -> x1, other arithmetic: 406 us -> 2.56 us
    pallas_call x0 -> x2, Pallas kernels: none -> 97.6 us  [the longest x1 93 us: form_beams(): pl.pallas_call(functools.partial(beam_kernel, scale=scale), out_shape=jax...]
    dot_general x26 -> x0, matrix products: 52.1 us -> none  [the longest x24 48.5 us: group_beams(): jnp.einsum('kfc,kcb->kfb', stacked_left, steering, preferred_element_type...]
    all_to_all x0 -> x1, waiting for transfers between devices: none -> 29.2 us  [on_device(): received = lax.all_to_all(rows, 'chan', 0, 0)]
    slice x8 -> x1, local copies, waits for them, and re-layouts: 15.2 us -> 0.91 us  [on_device(): waveform[:, :hop_length]]
    select_n x24 -> x0, other arithmetic: 13.5 us -> none  [group_beams(): reduced = jnp.mod(offsets, phase_steps)]
  transfers between devices with their start and end apart: 2 -> 2, of which waited for: 1 -> 1; matrix products, arithmetic and copies ran while one was open for 0% -> 2% of each run, Pallas kernels for 0% -> 0%
where the time goes in v1:
time: 142 us; the launch traced here: 141 us
  Pallas kernels  97.6 us (69%)
  waiting for transfers between devices  29.2 us (21%)
  starting transfers between devices  8.54 us (6%)
  local copies, waits for them, and re-layouts  3.1 us (2%)
  other arithmetic  2.63 us (2%)
    pallas_call x1, Pallas kernels, form_beams(): pl.pallas_call(functools.partial(beam_kernel, scale=scale), out_shape=jax...  93 us
    all_to_all x1, waiting for transfers between devices, on_device(): received = lax.all_to_all(rows, 'chan', 0, 0)  29.2 us
    all_to_all x1, starting transfers between devices, on_device(): received = lax.all_to_all(rows, 'chan', 0, 0)  7.25 us
    pallas_call x1, Pallas kernels, spectra_rows(): pl.pallas_call(spectra_kernel, out_shape=jax.ShapeDtypeStruct((bin_count,...  4.61 us
  transfers between devices with their start and end apart: 2, of which 1 were waited for; matrix products, arithmetic and copies ran while one was open for 2% of the time, Pallas kernels for 0%

profile of v1, /device:TPU:0, one launch (start us, length us, event | category | flops | bytes accessed | tf_op | source)
XLA Modules:
  0.0 141.1 jit_solution(16281994252176131059)
XLA Ops:
  0.0 0.9 slice.3
  0.9 1.3 collective-permute-start
  2.3 2.6 %multiply_convert_fusion.1 = (bf16[96,1024]{1,0:T(8,128)(2,1)S(1)}, bf16[96,1024]{1,0:T(8,128)(2,1)S(1)}) fusion(s32[96]{0:T(128)} %param.7, f32[1024]{0:T(1024)S(1)} %get-tuple-element.7, f32[1024]{0:T(1024)S(1)} %get-tuple-element.8), kind=kLoop, calls=%fused_computation.8 | loop fusion | flops 1966080 | bytes 401792 | tf_op jit(solution)/shard_map/convert
  4.9 0.0 collective-permute-done.next_ref
  4.9 0.0 copy-start
  4.9 1.9 %copy-done = bf16[128,12288]{1,0:T(8,128)(2,1)S(1)} copy-done((bf16[128,12288]{1,0:T(8,128)(2,1)S(1)}, bf16[128,12288]{1,0:T(8,128)(2,1)}, u32[]{:S(2)}) %copy-start) | copy-done | bytes 3145752
  6.8 0.0 copy-start.3
  6.8 0.0 copy-start.2
  6.8 0.0 copy-start.1
  6.8 4.6 %shard_map.46 = bf16[96,48,128]{2,1,0:T(8,128)(2,1)} custom-call(bf16[192,1024]{1,0:T(8,128)(2,1)S(1)} %pad_maximum_fusion.table_ref, bf16[128,12288]{1,0:T(8,128)(2,1)S(1)} %copy-done, bf16[128,512]{1,0:T(8,128)(2,1)S(1)} %collective-permute-done.next_ref), custom_call_target="tpu_custom_call" | custom-call | tf_op jit(solution)/shard_map/pallas_call | solution.py:61
  11.4 7.2 %all-to-all-start = ((bf16[8,12,48,128]{3,2,1,0:T(8,128)(2,1)}), bf16[8,12,48,128]{3,2,1,0:T(8,128)(2,1)S(1)}, u32[]{:S(2)}, u32[]{:S(2)}) async-start(bf16[8,12,48,128]{3,2,1,0:T(8,128)(2,1)} %bitcast.1), calls=%async_computation | async-start | bytes 2359296 | tf_op jit(solution)/shard_map/all_to_all | solution.py:146
  18.6 0.0 copy-done.3
  18.6 0.1 dynamic_slice.3.bins_ref
  18.7 0.0 copy-done.2
  18.7 0.2 copy.5
  18.9 29.2 %all-to-all-done.x_ref = bf16[8,12,48,128]{3,2,1,0:T(8,128)(2,1)S(1)} async-done(((bf16[8,12,48,128]{3,2,1,0:T(8,128)(2,1)}), bf16[8,12,48,128]{3,2,1,0:T(8,128)(2,1)S(1)}, u32[]{:S(2)}, u32[]{:S(2)}) %all-to-all-start) | async-done | bytes 1179680 | tf_op jit(solution)/shard_map/all_to_all | solution.py:146
  48.1 0.0 copy-done.1
  48.1 93.0 %shard_map.47 = f32[12,48,2048]{2,1,0:T(8,128)} custom-call(s32[12]{0:T(128)S(1)} %dynamic_slice.3.bins_ref, s32[1024,2]{1,0:T(8,128)S(1)} %bitcast.3, s32[2,2048]{1,0:T(2,128)S(1)} %copy-done.1, bf16[8,12,48,128]{3,2,1,0:T(8,128)(2,1)S(1)} %all-to-all-done.x_ref), custom_call_target="tpu_custom_call" | custom-call | tf_op jit(solution)/shard_map/pallas_call | solution.py:111
  (2 shorter events, 0.1 us)
Async XLA Ops:
  0.9 3.9 %collective-permute-start = (bf16[128,512]{1,0:T(8,128)(2,1)S(1)}, bf16[128,512]{1,0:T(8,128)(2,1)S(1)}, u32[]{:S(2)}, u32[]{:S(2)}) collective-permute-start(bf16[128,512]{1,0:T(8,128)(2,1)S(1)} %slice.3), channel_id=1, source_target_pairs={{1,0},{2,1},{3,2},{5,4},{6,5},{7,6},{9,8},{10,9},{11,10},{13,12},{... | collective-permute-start | bytes 393224 | tf_op jit(solution)/shard_map/ppermute | solution.py:140
  4.9 1.9 %copy-start = (bf16[128,12288]{1,0:T(8,128)(2,1)S(1)}, bf16[128,12288]{1,0:T(8,128)(2,1)}, u32[]{:S(2)}) copy-start(bf16[128,12288]{1,0:T(8,128)(2,1)} %wave_ref.1) | copy-start | bytes 9437188
  6.8 11.9 %copy-start.3 = (s32[96]{0:T(128)S(1)}, s32[96]{0:T(128)}, u32[]{:S(2)}) copy-start(s32[96]{0:T(128)} %param.7) | copy-start | bytes 1156
  6.8 12.0 %copy-start.2 = (s32[2,1024]{1,0:T(2,128)S(1)}, s32[2,1024]{1,0:T(2,128)}, u32[]{:S(2)}) copy-start(s32[2,1024]{1,0:T(2,128)} %param.5) | copy-start | bytes 24580
  6.8 41.3 %copy-start.1 = (s32[2,2048]{1,0:T(2,128)S(1)}, s32[2,2048]{1,0:T(2,128)}, u32[]{:S(2)}) copy-start(s32[2,2048]{1,0:T(2,128)} %directions_ref.1) | copy-start | bytes 49156
  11.4 36.7 %all-to-all-start = ((bf16[8,12,48,128]{3,2,1,0:T(8,128)(2,1)}), bf16[8,12,48,128]{3,2,1,0:T(8,128)(2,1)S(1)}, u32[]{:S(2)}, u32[]{:S(2)}) async-start(bf16[8,12,48,128]{3,2,1,0:T(8,128)(2,1)} %bitcast.1), calls=%async_computation | async-start | bytes 2359296 | tf_op jit(solution)/shard_map/all_to_all | solution.py:146

commit v2 on v1

--- a/solution.py
+++ b/solution.py
@@ -130,6 +130,117 @@
     )(own_bins, coords.T, directions, received)
 
 
+def steering_kernel(bins_ref, coords_ref, directions_ref, out_ref, offsets_ref):
+    sine, cosine = half_angle_fit()
+    channels = out_ref.shape[2]
+    step = 16
+
+    @pl.when(pl.program_id(1) == 0)
+    def _():
+        @pl.loop(0, channels, step=step)
+        def _(at):
+            piece = pl.ds(at, step)
+            offsets_ref[piece, :] = (
+                coords_ref[piece, 0:1] * directions_ref[0:1, :] + coords_ref[piece, 1:2] * directions_ref[1:2, :]
+            )
+
+    turn = bins_ref[pl.program_id(1)] * (2**32 // PHASE_STEPS)
+    for at in range(0, channels, step):
+        x = (offsets_ref[at : at + step, :] * turn).astype(jnp.float32) * 2.0**-32
+        w = x * x
+        s = ((sine[2] * w + sine[1]) * w + sine[0]) * x
+        c = ((cosine[3] * w + cosine[2]) * w + cosine[1]) * w + cosine[0]
+        out_ref[0, 0, at : at + step, :] = (1.0 - s * s).astype(jnp.bfloat16)
+        out_ref[0, 1, at : at + step, :] = (s * c).astype(jnp.bfloat16)
+
+
+def make_steering(some_bins, coords, directions):
+    count = some_bins.shape[0]
+    channels, beams = coords.shape[1], directions.shape[1]
+    tile = min(BEAM_TILE, beams)
+    values = count * channels * beams
+    return pl.pallas_call(
+        steering_kernel,
+        out_shape=jax.ShapeDtypeStruct((count, 2, channels, beams), jnp.bfloat16),
+        grid_spec=pltpu.PrefetchScalarGridSpec(
+            num_scalar_prefetch=1,
+            grid=(beams // tile, count),
+            in_specs=[
+                pl.BlockSpec((channels, 2), lambda j, f, s: (0, 0)),
+                pl.BlockSpec((2, tile), lambda j, f, s: (0, j)),
+            ],
+            out_specs=pl.BlockSpec((1, 2, channels, tile), lambda j, f, s: (f, 0, 0, j)),
+            scratch_shapes=[pltpu.VMEM((channels, tile), jnp.int32)],
+        ),
+        compiler_params=pltpu.CompilerParams(vmem_limit_bytes=32 * 2**20),
+        cost_estimate=pl.CostEstimate(flops=20 * values, bytes_accessed=4 * values, transcendentals=2 * values),
+    )(some_bins, coords.T, directions)
+
+
+def product_kernel(at_ref, steering_ref, own_ref, other_ref, own_out_ref, other_out_ref, *, scale):
+    sources, _, rows, _ = own_ref.shape
+    frames = rows // 2
+    left = jnp.concatenate(
+        [jnp.concatenate([ref[k, 0] for k in range(sources)], axis=1) for ref in (own_ref, other_ref)], axis=0
+    )
+    by_cos = jnp.dot(left, steering_ref[0, 0], preferred_element_type=jnp.float32)
+    by_sin = jnp.dot(left, steering_ref[0, 1], preferred_element_type=jnp.float32)
+    for k, ref in enumerate((own_out_ref, other_out_ref)):
+        real, imag = slice(k * rows, k * rows + frames), slice(k * rows + frames, (k + 1) * rows)
+        ref[0, :frames, :] = (by_cos[real] - by_sin[imag]) * scale
+        ref[0, frames:, :] = (by_cos[imag] + by_sin[real]) * scale
+
+
+def multiply(first_own, first, count, steering, received, partner):
+    sources, _, rows, width = received.shape
+    channels, beams = steering.shape[2:]
+    tile = min(BEAM_TILE, beams)
+    block = (sources, 1, rows, width)
+    out = jax.ShapeDtypeStruct((count, rows, beams), jnp.float32)
+    out_spec = pl.BlockSpec((1, rows, tile), lambda f, j, s: (f, 0, j))
+    return pl.pallas_call(
+        functools.partial(product_kernel, scale=1.0 / math.sqrt(channels)),
+        out_shape=(out, out),
+        grid_spec=pltpu.PrefetchScalarGridSpec(
+            num_scalar_prefetch=1,
+            grid=(count, beams // tile),
+            in_specs=[
+                pl.BlockSpec((1, 2, channels, tile), lambda f, j, s: (first + f, 0, 0, j)),
+                pl.BlockSpec(block, lambda f, j, s: (0, s[0] + first + f, 0, 0)),
+                pl.BlockSpec(block, lambda f, j, s: (0, first + f, 0, 0)),
+            ],
+            out_specs=(out_spec, out_spec),
+        ),
+        compiler_params=pltpu.CompilerParams(vmem_limit_bytes=32 * 2**20),
+        cost_estimate=pl.CostEstimate(
+            flops=8 * count * rows * channels * beams,
+            bytes_accessed=count * beams * (4 * channels + 8 * rows),
+            transcendentals=0,
+        ),
+    )(first_own[None], steering, received, partner)
+
+
+def shared_beams(own_bins, coords, directions, rows):
+    tm_count = lax.axis_size("tm")
+    core = lax.rem(lax.axis_index("tm"), 2)
+    swap = [(i, i ^ 1) for i in range(tm_count)]
+    half = own_bins.shape[0] // 2
+    received = lax.all_to_all(rows, "chan", 0, 0)
+    some_bins = lax.dynamic_slice_in_dim(own_bins, core * half, half, 0)
+    steering = make_steering(some_bins, coords, directions)
+    partner = lax.ppermute(lax.dynamic_slice_in_dim(received, (1 - core) * half, half, 1), "tm", swap)
+    kept, swapped = [], []
+    first = 0
+    for count in (half - half // 2, half // 2):
+        if count == 0:
+            continue
+        own, other = multiply(core * half, first, count, steering, received, partner)
+        kept.append(own)
+        swapped.append(lax.ppermute(other, "tm", swap))
+        first += count
+    return jnp.where(core == 0, jnp.concatenate(kept + swapped), jnp.concatenate(swapped + kept))
+
+
 def on_device(waveform, coords, directions, bins):
     channels_dev = waveform.shape[0]
     hop_length = FL // 2
@@ -143,9 +254,13 @@
     table = dft_table(bins, FL)
     rows = spectra_rows(table, waveform, following)
     rows = rows.reshape(chan_count, bins_dev, 2 * frames_dev, channels_dev)
-    received = lax.all_to_all(rows, "chan", 0, 0)
+    coords, rows = lax.optimization_barrier((coords, rows))
     own_bins = lax.dynamic_slice_in_dim(bins, lax.axis_index("chan") * bins_dev, bins_dev, 0)
-    beams = form_beams(own_bins, coords, directions, received)
+    if bins_dev % 2 == 0 and tm_count % 2 == 0:
+        beams = shared_beams(own_bins, coords, directions, rows)
+    else:
+        received = lax.all_to_all(rows, "chan", 0, 0)
+        beams = form_beams(own_bins, coords, directions, received)
     return beams.reshape(bins_dev, 2, frames_dev, directions.shape[1])
 
 

time: 142 us -> 141 us (level)
  Pallas kernels: 97.6 us -> 87.6 us
  other arithmetic: 2.63 us -> 6.82 us
  waiting for transfers between devices: 29.2 us -> 32.2 us
    pallas_call x1 -> x3, Pallas kernels: 93 us -> 83 us  [the longest x1 53.5 us: make_steering(): pl.pallas_call(steering_kernel, out_shape=jax.ShapeDtypeStruct((count, 2,...]
    select_n x0 -> x1, other arithmetic: none -> 4.19 us  [shared_beams(): jnp.where(core == 0, jnp.concatenate(kept + swapped), jnp.concatenate(swa...]
    ppermute x0 -> x3, waiting for transfers between devices: none -> 2.69 us  [the longest x2 2.68 us: shared_beams(): swapped.append(lax.ppermute(other, 'tm', swap))]
    unnamed x9 -> x10, local copies, waits for them, and re-layouts: 2.12 us -> 2.94 us
  transfers between devices with their start and end apart: 2 -> 5, of which waited for: 1 -> 2; matrix products, arithmetic and copies ran while one was open for 2% -> 2% of each run, Pallas kernels for 0% -> 48%
where the time goes in v2:
time: 141 us
  Pallas kernels  87.6 us (62%)
  waiting for transfers between devices  32.2 us (23%)
  starting transfers between devices  9.87 us (7%)
  other arithmetic  6.82 us (5%)
  local copies, waits for them, and re-layouts  4.19 us (3%)
    pallas_call x1, Pallas kernels, make_steering(): pl.pallas_call(steering_kernel, out_shape=jax.ShapeDtypeStruct((count, 2,...  53.5 us
    pallas_call x2, Pallas kernels, multiply(): pl.pallas_call(functools.partial(product_kernel, scale=1.0 / math.sqrt(ch...  29.5 us
    all_to_all x1, waiting for transfers between devices, shared_beams(): received = lax.all_to_all(rows, 'chan', 0, 0)  29.5 us
    all_to_all x1, starting transfers between devices, shared_beams(): received = lax.all_to_all(rows, 'chan', 0, 0)  7.26 us
    pallas_call x1, Pallas kernels, spectra_rows(): pl.pallas_call(spectra_kernel, out_shape=jax.ShapeDtypeStruct((bin_count,...  4.61 us
    select_n x1, other arithmetic, shared_beams(): jnp.where(core == 0, jnp.concatenate(kept + swapped), jnp.concatenate(swa...  4.19 us
    unnamed x10, local copies, waits for them, and re-layouts  2.94 us
  transfers between devices with their start and end apart: 5, of which 2 were waited for; matrix products, arithmetic and copies ran while one was open for 2% of the time, Pallas kernels for 48%

profile of v2, /device:TPU:0, one launch (start us, length us, event | category | flops | bytes accessed | tf_op | source)
XLA Modules:
  0.0 140.7 jit_solution(7865635945271932640)
XLA Ops:
  0.0 0.9 slice.3
  0.9 1.3 collective-permute-start
  2.3 2.6 %multiply_convert_fusion.1 = (bf16[96,1024]{1,0:T(8,128)(2,1)S(1)}, bf16[96,1024]{1,0:T(8,128)(2,1)S(1)}) fusion(s32[96]{0:T(128)} %param.7, f32[1024]{0:T(1024)S(1)} %get-tuple-element.19, f32[1024]{0:T(1024)S(1)} %get-tuple-element.20), kind=kLoop, calls=%fused_computation.9 | loop fusion | flops 1966080 | bytes 401792 | tf_op jit(solution)/shard_map/convert
  4.8 0.0 copy-start.4
  4.8 0.0 copy-start.3
  4.9 0.0 copy-start.2
  4.9 0.0 collective-permute-done.next_ref
  4.9 0.0 copy-start
  4.9 1.9 %copy-done = bf16[128,12288]{1,0:T(8,128)(2,1)S(1)} copy-done((bf16[128,12288]{1,0:T(8,128)(2,1)S(1)}, bf16[128,12288]{1,0:T(8,128)(2,1)}, u32[]{:S(2)}) %copy-start) | copy-done | bytes 3145752
  6.8 4.6 %shard_map.46 = bf16[96,48,128]{2,1,0:T(8,128)(2,1)} custom-call(bf16[192,1024]{1,0:T(8,128)(2,1)S(1)} %pad_maximum_fusion.table_ref, bf16[128,12288]{1,0:T(8,128)(2,1)S(1)} %copy-done, bf16[128,512]{1,0:T(8,128)(2,1)S(1)} %collective-permute-done.next_ref), custom_call_target="tpu_custom_call" | custom-call | tf_op jit(solution)/shard_map/pallas_call | solution.py:61
  11.4 7.3 %all-to-all-start = ((bf16[8,12,48,128]{3,2,1,0:T(8,128)(2,1)}), bf16[8,12,48,128]{3,2,1,0:T(8,128)(2,1)S(1)}, u32[]{:S(2)}, u32[]{:S(2)}) async-start(bf16[8,12,48,128]{3,2,1,0:T(8,128)(2,1)} %bitcast.1), calls=%async_computation | async-start | bytes 2359296 | tf_op jit(solution)/shard_map/all_to_all | solution.py:228
  18.7 29.5 %all-to-all-done.own_ref = bf16[8,12,48,128]{3,2,1,0:T(8,128)(2,1)S(1)} async-done(((bf16[8,12,48,128]{3,2,1,0:T(8,128)(2,1)}), bf16[8,12,48,128]{3,2,1,0:T(8,128)(2,1)S(1)}, u32[]{:S(2)}, u32[]{:S(2)}) %all-to-all-start) | async-done | bytes 1179680 | tf_op jit(solution)/shard_map/all_to_all | solution.py:228
  48.2 0.8 collective-permute-start.1
  49.0 0.0 copy-done.4
  49.0 0.1 dynamic_slice.10.bins_ref
  49.1 0.0 copy-done.3
  49.1 0.2 copy.5
  49.3 0.0 copy-done.2
  49.3 53.5 %shard_map.47.steering_ref = bf16[6,2,1024,2048]{3,2,1,0:T(8,128)(2,1)} custom-call(s32[6]{0:T(128)S(1)} %dynamic_slice.10.bins_ref, s32[1024,2]{1,0:T(8,128)S(1)} %bitcast.7, s32[2,2048]{1,0:T(2,128)S(1)} %copy-done.2), custom_call_target="tpu_custom_call" | custom-call | flops 251658240 | bytes 50331648 | tf_op jit(solution)/shard_map/pallas_call | solution.py:162
  102.8 0.0 collective-permute-done.1.other_ref
  102.8 14.8 %shard_map.48 = (f32[3,48,2048]{2,1,0:T(8,128)S(1)}, f32[3,48,2048]{2,1,0:T(8,128)}) custom-call(s32[1]{0:T(128)} %bitcast.at_ref, bf16[6,2,1024,2048]{3,2,1,0:T(8,128)(2,1)} %shard_map.47.steering_ref, bf16[8,12,48,128]{3,2,1,0:T(8,128)(2,1)S(1)} %all-to-all-done.own_ref, bf16[8,6,48,128]{3,2,1,0:T(8,128)(2,1)S(1)} %collective-permute-done.1.other_ref), custom_call_target="tpu_custom_call" | custom-call | flops 2415919104 | bytes 27525120 | tf_op jit(solution)/shard_map/pallas_call | solution.py:201
  117.6 0.0 collective-permute-start.2
  117.6 14.8 %shard_map.49 = (f32[3,48,2048]{2,1,0:T(8,128)S(1)}, f32[3,48,2048]{2,1,0:T(8,128)}) custom-call(s32[1]{0:T(128)} %bitcast.at_ref, bf16[6,2,1024,2048]{3,2,1,0:T(8,128)(2,1)} %shard_map.47.steering_ref, bf16[8,12,48,128]{3,2,1,0:T(8,128)(2,1)S(1)} %all-to-all-done.own_ref, bf16[8,6,48,128]{3,2,1,0:T(8,128)(2,1)S(1)} %collective-permute-done.1.other_ref), custom_call_target="tpu_custom_call" | custom-call | flops 2415919104 | bytes 27525120 | tf_op jit(solution)/shard_map/pallas_call | solution.py:201
  132.4 0.0 copy-start.1
  132.4 1.0 copy-done.1
  133.4 0.5 collective-permute-start.3
  133.9 0.0 collective-permute-done.2
  133.9 2.7 %collective-permute-done.3 = f32[3,48,2048]{2,1,0:T(8,128)S(1)} collective-permute-done((f32[3,48,2048]{2,1,0:T(8,128)}, f32[3,48,2048]{2,1,0:T(8,128)S(1)}, u32[]{:S(2)}, u32[]{:S(2)}) %collective-permute-start.3) | collective-permute-done | bytes 1179680 | tf_op jit(solution)/shard_map/ppermute | solution.py:239
  136.5 4.2 %maximum_select_fusion = f32[12,2,24,2048]{3,2,1,0:T(8,128)} fusion(f32[3,2,24,2048]{3,2,1,0:T(8,128)S(1)} %bitcast.10, f32[3,2,24,2048]{3,2,1,0:T(8,128)} %bitcast.5, f32[3,2,24,2048]{3,2,1,0:T(8,128)} %bitcast.9, f32[3,2,24,2048]{3,2,1,0:T(8,128)S(1)} %bitcast.8, pred[]{:T(512)S(6)} %eq.5), kind=kLoop, calls=%fused_computation | loop fusion | flops 8257536 | bytes 9437185 | tf_op jit(solution)/shard_map/jit(_where)/select_n | solution.py:241
  (3 shorter events, 0.1 us)
Async XLA Ops:
  0.9 4.0 %collective-permute-start = (bf16[128,512]{1,0:T(8,128)(2,1)S(1)}, bf16[128,512]{1,0:T(8,128)(2,1)S(1)}, u32[]{:S(2)}, u32[]{:S(2)}) collective-permute-start(bf16[128,512]{1,0:T(8,128)(2,1)S(1)} %slice.3), channel_id=1, source_target_pairs={{1,0},{2,1},{3,2},{5,4},{6,5},{7,6},{9,8},{10,9},{11,10},{13,12},{... | collective-permute-start | bytes 393224 | tf_op jit(solution)/shard_map/ppermute | solution.py:251
  4.8 44.2 %copy-start.4 = (s32[96]{0:T(128)S(1)}, s32[96]{0:T(128)}, u32[]{:S(2)}) copy-start(s32[96]{0:T(128)} %param.7) | copy-start | bytes 1156
  4.8 44.3 %copy-start.3 = (s32[2,1024]{1,0:T(2,128)S(1)}, s32[2,1024]{1,0:T(2,128)}, u32[]{:S(2)}) copy-start(s32[2,1024]{1,0:T(2,128)} %param.5) | copy-start | bytes 24580
  4.9 44.5 %copy-start.2 = (s32[2,2048]{1,0:T(2,128)S(1)}, s32[2,2048]{1,0:T(2,128)}, u32[]{:S(2)}) copy-start(s32[2,2048]{1,0:T(2,128)} %directions_ref.1) | copy-start | bytes 49156
  4.9 1.9 %copy-start = (bf16[128,12288]{1,0:T(8,128)(2,1)S(1)}, bf16[128,12288]{1,0:T(8,128)(2,1)}, u32[]{:S(2)}) copy-start(bf16[128,12288]{1,0:T(8,128)(2,1)} %wave_ref.1) | copy-start | bytes 9437188
  11.4 36.7 %all-to-all-start = ((bf16[8,12,48,128]{3,2,1,0:T(8,128)(2,1)}), bf16[8,12,48,128]{3,2,1,0:T(8,128)(2,1)S(1)}, u32[]{:S(2)}, u32[]{:S(2)}) async-start(bf16[8,12,48,128]{3,2,1,0:T(8,128)(2,1)} %bitcast.1), calls=%async_computation | async-start | bytes 2359296 | tf_op jit(solution)/shard_map/all_to_all | solution.py:228
  48.2 54.6 %collective-permute-start.1 = (bf16[8,6,48,128]{3,2,1,0:T(8,128)(2,1)S(1)}, bf16[8,6,48,128]{3,2,1,0:T(8,128)(2,1)S(1)}, u32[]{:S(2)}, u32[]{:S(2)}) collective-permute-start(bf16[8,6,48,128]{3,2,1,0:T(8,128)(2,1)S(1)} %constant_dynamic-slice_fusion), channel_id=1, source_target_pairs={{0,1},{1,0},{2,3},{3,2},{4,5},{5,4},{6,7},{7,6},{8,9},{9,8},{10,11... | collective-permute-start | bytes 1769480 | tf_op jit(solution)/shard_map/ppermute | solution.py:231
  117.6 16.3 %collective-permute-start.2 = (f32[3,48,2048]{2,1,0:T(8,128)}, f32[3,48,2048]{2,1,0:T(8,128)}, u32[]{:S(2)}, u32[]{:S(2)}) collective-permute-start(f32[3,48,2048]{2,1,0:T(8,128)} %get-tuple-element.15), channel_id=1, source_target_pairs={{0,1},{1,0},{2,3},{3,2},{4,5},{5,4},{6,7},{7,6},{8,9},{9,8},{10,11... | collective-permute-start | bytes 3538952 | tf_op jit(solution)/shard_map/ppermute | solution.py:239
  132.4 1.0 copy-start.1
  133.4 3.2 %collective-permute-start.3 = (f32[3,48,2048]{2,1,0:T(8,128)}, f32[3,48,2048]{2,1,0:T(8,128)S(1)}, u32[]{:S(2)}, u32[]{:S(2)}) collective-permute-start(f32[3,48,2048]{2,1,0:T(8,128)} %get-tuple-element.16), channel_id=1, source_target_pairs={{0,1},{1,0},{2,3},{3,2},{4,5},{5,4},{6,7},{7,6},{8,9},{9,8},{10,11... | collective-permute-start | bytes 3538952 | tf_op jit(solution)/shard_map/ppermute | solution.py:239

commit v3 on v2

--- a/solution.py
+++ b/solution.py
@@ -21,6 +21,11 @@
     sine = np.polynomial.polynomial.polyfit(w, np.sqrt(2) * np.sin(np.pi * r) / r, 2)
     cosine = np.polynomial.polynomial.polyfit(w, np.sqrt(2) * np.cos(np.pi * r), 3)
     return [float(c) for c in sine], [float(c) for c in cosine]
+
+
+def nearest_rest(turns):
+    anchor = jnp.float32(1.5 * 2**23)
+    return turns - ((turns + anchor) - anchor)
 
 
 def dft_table(bins, frame_length):
@@ -66,29 +71,20 @@
     )(table, waveform, following)
 
 
-def beam_kernel(bins_ref, coords_ref, directions_ref, x_ref, out_ref, offsets_ref, cos_ref, sin_ref, *, scale):
+def beam_kernel(bins_ref, offsets_ref, x_ref, out_ref, cos_ref, sin_ref, *, scale):
     sine, cosine = half_angle_fit()
     sources, _, rows, width = x_ref.shape
     channels = sources * width
     step = 16
 
-    @pl.when(pl.program_id(1) == 0)
-    def _():
-        @pl.loop(0, channels, step=step)
-        def _(at):
-            piece = pl.ds(at, step)
-            offsets_ref[piece, :] = (
-                coords_ref[piece, 0:1] * directions_ref[0:1, :] + coords_ref[piece, 1:2] * directions_ref[1:2, :]
-            )
-
-    turn = bins_ref[pl.program_id(1)] * (2**32 // PHASE_STEPS)
+    turn = bins_ref[pl.program_id(1)] .astype(jnp.float32)
     frames = rows // 2
     by_cos = jnp.zeros((rows, out_ref.shape[2]), jnp.float32)
     by_sin = jnp.zeros((rows, out_ref.shape[2]), jnp.float32)
     group = 2
     for first in range(0, sources, group):
         for at in range(first * width, (first + group) * width, step):
-            x = (offsets_ref[at : at + step, :] * turn).astype(jnp.float32) * 2.0**-32
+            x = nearest_rest(offsets_ref[at : at + step, :] * turn)
             w = x * x
             s = ((sine[2] * w + sine[1]) * w + sine[0]) * x
             c = ((cosine[3] * w + cosine[2]) * w + cosine[1]) * w + cosine[0]
@@ -102,10 +98,10 @@
     out_ref[0, frames:, :] = (by_cos[frames:] + by_sin[:frames]) * scale
 
 
-def form_beams(own_bins, coords, directions, received):
+def form_beams(own_bins, offsets, received):
     sources, bins_dev, rows, width = received.shape
     channels = sources * width
-    beams = directions.shape[1]
+    beams = offsets.shape[1]
     tile = min(BEAM_TILE, beams)
     scale = 1.0 / math.sqrt(channels)
     return pl.pallas_call(
@@ -115,66 +111,53 @@
             num_scalar_prefetch=1,
             grid=(beams // tile, bins_dev),
             in_specs=[
-                pl.BlockSpec((channels, 2), lambda j, f, s: (0, 0)),
-                pl.BlockSpec((2, tile), lambda j, f, s: (0, j)),
+                pl.BlockSpec((channels, tile), lambda j, f, s: (0, j)),
                 pl.BlockSpec((sources, 1, rows, width), lambda j, f, s: (0, f, 0, 0)),
             ],
             out_specs=pl.BlockSpec((1, rows, tile), lambda j, f, s: (f, 0, j)),
             scratch_shapes=[
-                pltpu.VMEM((channels, tile), jnp.int32),
                 pltpu.VMEM((channels, tile), jnp.bfloat16),
                 pltpu.VMEM((channels, tile), jnp.bfloat16),
             ],
         ),
         compiler_params=pltpu.CompilerParams(vmem_limit_bytes=48 * 2**20),
-    )(own_bins, coords.T, directions, received)
-
-
-def steering_kernel(bins_ref, coords_ref, directions_ref, out_ref, offsets_ref):
+    )(own_bins, offsets, received)
+
+
+def steering_kernel(bins_ref, offsets_ref, out_ref):
     sine, cosine = half_angle_fit()
-    channels = out_ref.shape[2]
+    channels = out_ref.shape[3]
     step = 16
 
-    @pl.when(pl.program_id(1) == 0)
-    def _():
-        @pl.loop(0, channels, step=step)
-        def _(at):
-            piece = pl.ds(at, step)
-            offsets_ref[piece, :] = (
-                coords_ref[piece, 0:1] * directions_ref[0:1, :] + coords_ref[piece, 1:2] * directions_ref[1:2, :]
-            )
-
-    turn = bins_ref[pl.program_id(1)] * (2**32 // PHASE_STEPS)
+    turn = bins_ref[pl.program_id(1)] .astype(jnp.float32)
     for at in range(0, channels, step):
-        x = (offsets_ref[at : at + step, :] * turn).astype(jnp.float32) * 2.0**-32
+        x = nearest_rest(offsets_ref[at : at + step, :] * turn)
         w = x * x
         s = ((sine[2] * w + sine[1]) * w + sine[0]) * x
         c = ((cosine[3] * w + cosine[2]) * w + cosine[1]) * w + cosine[0]
-        out_ref[0, 0, at : at + step, :] = (1.0 - s * s).astype(jnp.bfloat16)
-        out_ref[0, 1, at : at + step, :] = (s * c).astype(jnp.bfloat16)
-
-
-def make_steering(some_bins, coords, directions):
+        out_ref[0, 0, 0, at : at + step, :] = (1.0 - s * s).astype(jnp.bfloat16)
+        out_ref[0, 0, 1, at : at + step, :] = (s * c).astype(jnp.bfloat16)
+
+
+def make_steering(some_bins, offsets):
     count = some_bins.shape[0]
-    channels, beams = coords.shape[1], directions.shape[1]
+    channels, beams = offsets.shape
     tile = min(BEAM_TILE, beams)
     values = count * channels * beams
     return pl.pallas_call(
         steering_kernel,
-        out_shape=jax.ShapeDtypeStruct((count, 2, channels, beams), jnp.bfloat16),
+        out_shape=jax.ShapeDtypeStruct((count, beams // tile, 2, channels, tile), jnp.bfloat16),
         grid_spec=pltpu.PrefetchScalarGridSpec(
             num_scalar_prefetch=1,
             grid=(beams // tile, count),
             in_specs=[
-                pl.BlockSpec((channels, 2), lambda j, f, s: (0, 0)),
-                pl.BlockSpec((2, tile), lambda j, f, s: (0, j)),
-            ],
-            out_specs=pl.BlockSpec((1, 2, channels, tile), lambda j, f, s: (f, 0, 0, j)),
-            scratch_shapes=[pltpu.VMEM((channels, tile), jnp.int32)],
+                pl.BlockSpec((channels, tile), lambda j, f, s: (0, j)),
+            ],
+            out_specs=pl.BlockSpec((1, 1, 2, channels, tile), lambda j, f, s: (f, j, 0, 0, 0)),
         ),
         compiler_params=pltpu.CompilerParams(vmem_limit_bytes=32 * 2**20),
         cost_estimate=pl.CostEstimate(flops=20 * values, bytes_accessed=4 * values, transcendentals=2 * values),
-    )(some_bins, coords.T, directions)
+    )(some_bins, offsets)
 
 
 def product_kernel(at_ref, steering_ref, own_ref, other_ref, own_out_ref, other_out_ref, *, scale):
@@ -183,8 +166,8 @@
     left = jnp.concatenate(
         [jnp.concatenate([ref[k, 0] for k in range(sources)], axis=1) for ref in (own_ref, other_ref)], axis=0
     )
-    by_cos = jnp.dot(left, steering_ref[0, 0], preferred_element_type=jnp.float32)
-    by_sin = jnp.dot(left, steering_ref[0, 1], preferred_element_type=jnp.float32)
+    by_cos = jnp.dot(left, steering_ref[0, 0, 0], preferred_element_type=jnp.float32)
+    by_sin = jnp.dot(left, steering_ref[0, 0, 1], preferred_element_type=jnp.float32)
     for k, ref in enumerate((own_out_ref, other_out_ref)):
         real, imag = slice(k * rows, k * rows + frames), slice(k * rows + frames, (k + 1) * rows)
         ref[0, :frames, :] = (by_cos[real] - by_sin[imag]) * scale
@@ -193,8 +176,8 @@
 
 def multiply(first_own, first, count, steering, received, partner):
     sources, _, rows, width = received.shape
-    channels, beams = steering.shape[2:]
-    tile = min(BEAM_TILE, beams)
+    _, tiles, _, channels, tile = steering.shape
+    beams = tiles * tile
     block = (sources, 1, rows, width)
     out = jax.ShapeDtypeStruct((count, rows, beams), jnp.float32)
     out_spec = pl.BlockSpec((1, rows, tile), lambda f, j, s: (f, 0, j))
@@ -205,7 +188,7 @@
             num_scalar_prefetch=1,
             grid=(count, beams // tile),
             in_specs=[
-                pl.BlockSpec((1, 2, channels, tile), lambda f, j, s: (first + f, 0, 0, j)),
+                pl.BlockSpec((1, 1, 2, channels, tile), lambda f, j, s: (first + f, j, 0, 0, 0)),
                 pl.BlockSpec(block, lambda f, j, s: (0, s[0] + first + f, 0, 0)),
                 pl.BlockSpec(block, lambda f, j, s: (0, first + f, 0, 0)),
             ],
@@ -220,15 +203,37 @@
     )(first_own[None], steering, received, partner)
 
 
-def shared_beams(own_bins, coords, directions, rows):
+def give_kernel(at_ref, received_ref, steering_ref, out_ref):
+    out_ref[...] = received_ref[...]
+
+
+def cut_for_other(first_bin, count, received, steering):
+    sources, _, rows, width = received.shape
+    block = (sources, 1, rows, width)
+    return pl.pallas_call(
+        give_kernel,
+        out_shape=jax.ShapeDtypeStruct((sources, count, rows, width), received.dtype),
+        grid_spec=pltpu.PrefetchScalarGridSpec(
+            num_scalar_prefetch=1,
+            grid=(count,),
+            in_specs=[
+                pl.BlockSpec(block, lambda f, s: (0, s[0] + f, 0, 0)),
+                pl.BlockSpec(memory_space=pl.ANY),
+            ],
+            out_specs=pl.BlockSpec(block, lambda f, s: (0, f, 0, 0)),
+        ),
+    )(first_bin[None], received, steering)
+
+
+def shared_beams(own_bins, offsets, rows):
     tm_count = lax.axis_size("tm")
     core = lax.rem(lax.axis_index("tm"), 2)
     swap = [(i, i ^ 1) for i in range(tm_count)]
     half = own_bins.shape[0] // 2
     received = lax.all_to_all(rows, "chan", 0, 0)
     some_bins = lax.dynamic_slice_in_dim(own_bins, core * half, half, 0)
-    steering = make_steering(some_bins, coords, directions)
-    partner = lax.ppermute(lax.dynamic_slice_in_dim(received, (1 - core) * half, half, 1), "tm", swap)
+    steering = make_steering(some_bins, offsets)
+    partner = lax.ppermute(cut_for_other((1 - core) * half, half, received, steering), "tm", swap)
     kept, swapped = [], []
     first = 0
     for count in (half - half // 2, half // 2):
@@ -255,12 +260,15 @@
     rows = spectra_rows(table, waveform, following)
     rows = rows.reshape(chan_count, bins_dev, 2 * frames_dev, channels_dev)
     coords, rows = lax.optimization_barrier((coords, rows))
+    offsets = (
+        coords[0][:, None] * directions[0][None, :] + coords[1][:, None] * directions[1][None, :]
+    ).astype(jnp.float32) * (1.0 / PHASE_STEPS)
     own_bins = lax.dynamic_slice_in_dim(bins, lax.axis_index("chan") * bins_dev, bins_dev, 0)
     if bins_dev % 2 == 0 and tm_count % 2 == 0:
-        beams = shared_beams(own_bins, coords, directions, rows)
+        beams = shared_beams(own_bins, offsets, rows)
     else:
         received = lax.all_to_all(rows, "chan", 0, 0)
-        beams = form_beams(own_bins, coords, directions, received)
+        beams = form_beams(own_bins, offsets, received)
     return beams.reshape(bins_dev, 2, frames_dev, directions.shape[1])
 
 

time: 141 us -> 103 us (0.73)
  waiting for transfers between devices: 32.2 us -> 4.89 us
  Pallas kernels: 87.6 us -> 73 us
  other arithmetic: 6.82 us -> 8.44 us
    all_to_all x1, waiting for transfers between devices: 29.5 us -> 0.01 us  [shared_beams(): received = lax.all_to_all(rows, 'chan', 0, 0)]
    pallas_call x1 -> x2, Pallas kernels: 53.5 us -> 39.6 us  [the longest x1 35.5 us: make_steering(): pl.pallas_call(steering_kernel, out_shape=jax.ShapeDtypeStruct((count, be...]
    ppermute x1, waiting for transfers between devices: 0.01 us -> 1.84 us  [shared_beams(): lax.ppermute(cut_for_other((1 - core) * half, half, received, steering),...]
    mul x0 -> x1, other arithmetic: none -> 1.67 us  [on_device(): (coords[0][:, None] * directions[0][None, :] + coords[1][:, None] * direc...]
    unnamed x10 -> x12, local copies, waits for them, and re-layouts: 2.94 us -> 4.18 us
  transfers between devices with their start and end apart: 5 -> 5, of which waited for: 2 -> 2; matrix products, arithmetic and copies ran while one was open for 2% -> 4% of each run, Pallas kernels for 48% -> 49%
where the time goes in v3:
time: 103 us
  Pallas kernels  73 us (71%)
  starting transfers between devices  11.1 us (11%)
  other arithmetic  8.44 us (8%)
  local copies, waits for them, and re-layouts  5.2 us (5%)
  waiting for transfers between devices  4.89 us (5%)
    pallas_call x1, Pallas kernels, make_steering(): pl.pallas_call(steering_kernel, out_shape=jax.ShapeDtypeStruct((count, be...  35.5 us
    pallas_call x2, Pallas kernels, multiply(): pl.pallas_call(functools.partial(product_kernel, scale=1.0 / math.sqrt(ch...  28.8 us
    all_to_all x1, starting transfers between devices, shared_beams(): received = lax.all_to_all(rows, 'chan', 0, 0)  7.26 us
    pallas_call x1, Pallas kernels, spectra_rows(): pl.pallas_call(spectra_kernel, out_shape=jax.ShapeDtypeStruct((bin_count,...  4.61 us
    unnamed x12, local copies, waits for them, and re-layouts  4.18 us
    select_n x1, other arithmetic, shared_beams(): jnp.where(core == 0, jnp.concatenate(kept + swapped), jnp.concatenate(swa...  4.14 us
    pallas_call x1, Pallas kernels, cut_for_other(): pl.pallas_call(give_kernel, out_shape=jax.ShapeDtypeStruct((sources, coun...  4.08 us
    ppermute x2, waiting for transfers between devices, shared_beams(): swapped.append(lax.ppermute(other, 'tm', swap))  3.04 us
  transfers between devices with their start and end apart: 5, of which 2 were waited for; matrix products, arithmetic and copies ran while one was open for 4% of the time, Pallas kernels for 49%

profile of v3, /device:TPU:0, one launch (start us, length us, event | category | flops | bytes accessed | tf_op | source)
XLA Modules:
  0.0 102.7 jit_solution(2390813281534298285)
XLA Ops:
  0.0 0.0 copy-start.5
  0.0 0.0 copy-start.4
  0.0 0.0 copy-start.3
  0.0 0.9 slice.15
  0.9 1.3 %collective-permute-start = (bf16[128,512]{1,0:T(8,128)(2,1)S(1)}, bf16[128,512]{1,0:T(8,128)(2,1)S(1)}, u32[]{:S(2)}, u32[]{:S(2)}) collective-permute-start(bf16[128,512]{1,0:T(8,128)(2,1)S(1)} %slice.15), channel_id=1, source_target_pairs={{1,0},{2,1},{3,2},{5,4},{6,5},{7,6},{9,8},{10,9},{11,10},{13,12},{... | collective-permute-start | bytes 393224 | tf_op jit(solution)/shard_map/ppermute | solution.py:256
  2.3 2.6 %multiply_convert_fusion.1 = (bf16[96,1024]{1,0:T(8,128)(2,1)S(1)}, bf16[96,1024]{1,0:T(8,128)(2,1)S(1)}) fusion(s32[96]{0:T(128)} %param.7, f32[1024]{0:T(1024)S(1)} %get-tuple-element.23, f32[1024]{0:T(1024)S(1)} %get-tuple-element.24), kind=kLoop, calls=%fused_computation.10 | loop fusion | flops 1966080 | bytes 401792 | tf_op jit(solution)/shard_map/convert
  4.9 0.0 collective-permute-done.next_ref
  4.9 0.0 copy-start.2
  4.9 1.9 %copy-done.2 = bf16[128,12288]{1,0:T(8,128)(2,1)S(1)} copy-done((bf16[128,12288]{1,0:T(8,128)(2,1)S(1)}, bf16[128,12288]{1,0:T(8,128)(2,1)}, u32[]{:S(2)}) %copy-start.2) | copy-done | bytes 3145752
  6.8 4.6 %shard_map.46 = bf16[96,48,128]{2,1,0:T(8,128)(2,1)} custom-call(bf16[192,1024]{1,0:T(8,128)(2,1)S(1)} %pad_maximum_fusion.table_ref, bf16[128,12288]{1,0:T(8,128)(2,1)S(1)} %copy-done.2, bf16[128,512]{1,0:T(8,128)(2,1)S(1)} %collective-permute-done.next_ref), custom_call_target="tpu_custom_call" | custom-call | tf_op jit(solution)/shard_map/pallas_call | solution.py:66
  11.4 7.3 %all-to-all-start = ((bf16[8,12,48,128]{3,2,1,0:T(8,128)(2,1)}), bf16[8,12,48,128]{3,2,1,0:T(8,128)(2,1)S(1)}, u32[]{:S(2)}, u32[]{:S(2)}) async-start(bf16[8,12,48,128]{3,2,1,0:T(8,128)(2,1)} %bitcast.1), calls=%async_computation | async-start | bytes 2359296 | tf_op jit(solution)/shard_map/all_to_all | solution.py:233
  18.7 0.0 copy-done.5
  18.7 0.1 dynamic_slice.7.bins_ref
  18.7 0.0 copy-done.3
  18.8 0.0 copy-done.4
  18.8 1.7 %convert_multiply_fusion.offsets_ref = f32[1024,2048]{1,0:T(8,128)S(1)} fusion(s32[2048]{0:T(1024)S(1)} %bitcast.14, s32[1024]{0:T(1024)S(1)} %bitcast.16, s32[2048]{0:T(1024)S(1)} %bitcast.13, s32[1024]{0:T(1024)S(1)} %bitcast.15), kind=kLoop, calls=%fused_computation | loop fusion | flops 10485760 | bytes 8413184 | tf_op jit(solution)/shard_map/mul | solution.py:263
  20.5 35.5 %shard_map.47.steering_ref = bf16[6,4,2,1024,512]{4,3,2,1,0:T(8,128)(2,1)} custom-call(s32[6]{0:T(128)S(1)} %dynamic_slice.7.bins_ref, f32[1024,2048]{1,0:T(8,128)S(1)} %convert_multiply_fusion.offsets_ref), custom_call_target="tpu_custom_call" | custom-call | flops 251658240 | bytes 50331648 | tf_op jit(solution)/shard_map/pallas_call | solution.py:147
  56.0 0.0 all-to-all-done.received_ref.own_ref
  56.0 0.0 copy-start
  56.0 1.0 copy-done
  57.0 4.1 %shard_map.48 = bf16[8,6,48,128]{3,2,1,0:T(8,128)(2,1)} custom-call(s32[1]{0:T(128)} %bitcast.6.at_ref, bf16[8,12,48,128]{3,2,1,0:T(8,128)(2,1)} %copy-done, bf16[6,4,2,1024,512]{4,3,2,1,0:T(8,128)(2,1)} %shard_map.47.steering_ref), custom_call_target="tpu_custom_call" | custom-call | tf_op jit(solution)/shard_map/pallas_call | solution.py:213
  61.1 1.9 %collective-permute-start.1 = (bf16[8,6,48,128]{3,2,1,0:T(8,128)(2,1)}, bf16[8,6,48,128]{3,2,1,0:T(8,128)(2,1)S(1)}, u32[]{:S(2)}, u32[]{:S(2)}) collective-permute-start(bf16[8,6,48,128]{3,2,1,0:T(8,128)(2,1)} %shard_map.48), channel_id=1, source_target_pairs={{0,1},{1,0},{2,3},{3,2},{4,5},{5,4},{6,7},{7,6},{8,9},{9,8},{10,11... | collective-permute-start | bytes 1769480 | tf_op jit(solution)/shard_map/ppermute | solution.py:236
  63.0 1.8 %collective-permute-done.1.other_ref = bf16[8,6,48,128]{3,2,1,0:T(8,128)(2,1)S(1)} collective-permute-done((bf16[8,6,48,128]{3,2,1,0:T(8,128)(2,1)}, bf16[8,6,48,128]{3,2,1,0:T(8,128)(2,1)S(1)}, u32[]{:S(2)}, u32[]{:S(2)}) %collective-permute-start.1) | collective-permute-done | bytes 589856 | tf_op jit(solution)/shard_map/ppermute | solution.py:236
  64.9 0.0 copy-start.1
  64.9 1.3 %copy-done.1 = bf16[8,12,48,128]{3,2,1,0:T(8,128)(2,1)S(1)} copy-done((bf16[8,12,48,128]{3,2,1,0:T(8,128)(2,1)S(1)}, bf16[8,12,48,128]{3,2,1,0:T(8,128)(2,1)}, u32[]{:S(2)}) %copy-start.1) | copy-done | bytes 1179672
  66.1 14.0 %shard_map.49 = (f32[3,48,2048]{2,1,0:T(8,128)S(1)}, f32[3,48,2048]{2,1,0:T(8,128)S(1)}) custom-call(s32[1]{0:T(128)} %bitcast.at_ref, bf16[6,4,2,1024,512]{4,3,2,1,0:T(8,128)(2,1)} %shard_map.47.steering_ref, bf16[8,12,48,128]{3,2,1,0:T(8,128)(2,1)S(1)} %copy-done.1, bf16[8,6,48,128]{3,2,1,0:T(8,128)(2,1)S(1)} %collective-permute-done.1.other_ref), custom_call_target="tpu_custom_call" | custom-call | flops 2415919104 | bytes 27525120 | tf_op jit(solution)/shard_map/pallas_call | solution.py:184
  80.2 0.4 collective-permute-start.2
  80.6 14.7 %shard_map.50 = (f32[3,48,2048]{2,1,0:T(8,128)S(1)}, f32[3,48,2048]{2,1,0:T(8,128)}) custom-call(s32[1]{0:T(128)} %bitcast.at_ref, bf16[6,4,2,1024,512]{4,3,2,1,0:T(8,128)(2,1)} %shard_map.47.steering_ref, bf16[8,12,48,128]{3,2,1,0:T(8,128)(2,1)S(1)} %copy-done.1, bf16[8,6,48,128]{3,2,1,0:T(8,128)(2,1)S(1)} %collective-permute-done.1.other_ref), custom_call_target="tpu_custom_call" | custom-call | flops 2415919104 | bytes 27525120 | tf_op jit(solution)/shard_map/pallas_call | solution.py:184
  95.3 0.1 collective-permute-start.3
  95.5 0.0 collective-permute-done.2
  95.5 3.0 %collective-permute-done.3 = f32[3,48,2048]{2,1,0:T(8,128)} collective-permute-done((f32[3,48,2048]{2,1,0:T(8,128)}, f32[3,48,2048]{2,1,0:T(8,128)}, u32[]{:S(2)}, u32[]{:S(2)}) %collective-permute-start.3) | collective-permute-done | bytes 1179680 | tf_op jit(solution)/shard_map/ppermute | solution.py:244
  98.5 4.1 %maximum_select_fusion = f32[12,2,24,2048]{3,2,1,0:T(8,128)} fusion(f32[3,2,24,2048]{3,2,1,0:T(8,128)} %bitcast.10, f32[3,2,24,2048]{3,2,1,0:T(8,128)} %bitcast.9, f32[3,2,24,2048]{3,2,1,0:T(8,128)S(1)} %bitcast.12, f32[3,2,24,2048]{3,2,1,0:T(8,128)S(1)} %bitcast.11, pred[]{:T(512)S(6)} %eq.5), kind=kLoop, calls=%fused_computation.1 | loop fusion | flops 8257536 | bytes 9437185 | tf_op jit(solution)/shard_map/jit(_where)/select_n | solution.py:246
  (4 shorter events, 0.1 us)
Async XLA Ops:
  0.0 18.7 %copy-start.5 = (s32[96]{0:T(128)S(1)}, s32[96]{0:T(128)}, u32[]{:S(2)}) copy-start(s32[96]{0:T(128)} %param.7) | copy-start | bytes 1156
  0.0 18.8 %copy-start.4 = (s32[2,1024]{1,0:T(2,128)S(1)}, s32[2,1024]{1,0:T(2,128)}, u32[]{:S(2)}) copy-start(s32[2,1024]{1,0:T(2,128)} %param.5) | copy-start | bytes 24580
  0.0 18.7 %copy-start.3 = (s32[2,2048]{1,0:T(2,128)S(1)}, s32[2,2048]{1,0:T(2,128)}, u32[]{:S(2)}) copy-start(s32[2,2048]{1,0:T(2,128)} %param.6) | copy-start | bytes 49156
  0.9 3.9 %collective-permute-start = (bf16[128,512]{1,0:T(8,128)(2,1)S(1)}, bf16[128,512]{1,0:T(8,128)(2,1)S(1)}, u32[]{:S(2)}, u32[]{:S(2)}) collective-permute-start(bf16[128,512]{1,0:T(8,128)(2,1)S(1)} %slice.15), channel_id=1, source_target_pairs={{1,0},{2,1},{3,2},{5,4},{6,5},{7,6},{9,8},{10,9},{11,10},{13,12},{... | collective-permute-start | bytes 393224 | tf_op jit(solution)/shard_map/ppermute | solution.py:256
  4.9 1.9 %copy-start.2 = (bf16[128,12288]{1,0:T(8,128)(2,1)S(1)}, bf16[128,12288]{1,0:T(8,128)(2,1)}, u32[]{:S(2)}) copy-start(bf16[128,12288]{1,0:T(8,128)(2,1)} %wave_ref.1) | copy-start | bytes 9437188
  11.4 44.6 %all-to-all-start = ((bf16[8,12,48,128]{3,2,1,0:T(8,128)(2,1)}), bf16[8,12,48,128]{3,2,1,0:T(8,128)(2,1)S(1)}, u32[]{:S(2)}, u32[]{:S(2)}) async-start(bf16[8,12,48,128]{3,2,1,0:T(8,128)(2,1)} %bitcast.1), calls=%async_computation | async-start | bytes 2359296 | tf_op jit(solution)/shard_map/all_to_all | solution.py:233
  56.0 1.0 copy-start
  61.1 3.8 %collective-permute-start.1 = (bf16[8,6,48,128]{3,2,1,0:T(8,128)(2,1)}, bf16[8,6,48,128]{3,2,1,0:T(8,128)(2,1)S(1)}, u32[]{:S(2)}, u32[]{:S(2)}) collective-permute-start(bf16[8,6,48,128]{3,2,1,0:T(8,128)(2,1)} %shard_map.48), channel_id=1, source_target_pairs={{0,1},{1,0},{2,3},{3,2},{4,5},{5,4},{6,7},{7,6},{8,9},{9,8},{10,11... | collective-permute-start | bytes 1769480 | tf_op jit(solution)/shard_map/ppermute | solution.py:236
  64.9 1.3 %copy-start.1 = (bf16[8,12,48,128]{3,2,1,0:T(8,128)(2,1)S(1)}, bf16[8,12,48,128]{3,2,1,0:T(8,128)(2,1)}, u32[]{:S(2)}) copy-start(bf16[8,12,48,128]{3,2,1,0:T(8,128)(2,1)} %copy-done) | copy-start | bytes 3538948
  80.2 15.3 %collective-permute-start.2 = (f32[3,48,2048]{2,1,0:T(8,128)S(1)}, f32[3,48,2048]{2,1,0:T(8,128)}, u32[]{:S(2)}, u32[]{:S(2)}) collective-permute-start(f32[3,48,2048]{2,1,0:T(8,128)S(1)} %get-tuple-element.15), channel_id=1, source_target_pairs={{0,1},{1,0},{2,3},{3,2},{4,5},{5,4},{6,7},{7,6},{8,9},{9,8},{10,11... | collective-permute-start | bytes 3538952 | tf_op jit(solution)/shard_map/ppermute | solution.py:244
  95.3 3.2 %collective-permute-start.3 = (f32[3,48,2048]{2,1,0:T(8,128)}, f32[3,48,2048]{2,1,0:T(8,128)}, u32[]{:S(2)}, u32[]{:S(2)}) collective-permute-start(f32[3,48,2048]{2,1,0:T(8,128)} %get-tuple-element.16), channel_id=1, source_target_pairs={{0,1},{1,0},{2,3},{3,2},{4,5},{5,4},{6,7},{7,6},{8,9},{9,8},{10,11... | collective-permute-start | bytes 3538952 | tf_op jit(solution)/shard_map/ppermute | solution.py:244

commit v4 on v3

--- a/solution.py
+++ b/solution.py
@@ -207,22 +207,22 @@
     out_ref[...] = received_ref[...]
 
 
-def cut_for_other(first_bin, count, received, steering):
+def cut_for_other(half_index, count, received, steering):
     sources, _, rows, width = received.shape
-    block = (sources, 1, rows, width)
+    block = (sources, count, rows, width)
     return pl.pallas_call(
         give_kernel,
         out_shape=jax.ShapeDtypeStruct((sources, count, rows, width), received.dtype),
         grid_spec=pltpu.PrefetchScalarGridSpec(
             num_scalar_prefetch=1,
-            grid=(count,),
-            in_specs=[
-                pl.BlockSpec(block, lambda f, s: (0, s[0] + f, 0, 0)),
+            grid=(1,),
+            in_specs=[
+                pl.BlockSpec(block, lambda f, s: (0, s[0], 0, 0)),
                 pl.BlockSpec(memory_space=pl.ANY),
             ],
-            out_specs=pl.BlockSpec(block, lambda f, s: (0, f, 0, 0)),
-        ),
-    )(first_bin[None], received, steering)
+            out_specs=pl.BlockSpec(block, lambda f, s: (0, 0, 0, 0)),
+        ),
+    )(half_index[None], received, steering)
 
 
 def shared_beams(own_bins, offsets, rows):
@@ -233,7 +233,7 @@
     received = lax.all_to_all(rows, "chan", 0, 0)
     some_bins = lax.dynamic_slice_in_dim(own_bins, core * half, half, 0)
     steering = make_steering(some_bins, offsets)
-    partner = lax.ppermute(cut_for_other((1 - core) * half, half, received, steering), "tm", swap)
+    partner = lax.ppermute(cut_for_other(1 - core, half, received, steering), "tm", swap)
     kept, swapped = [], []
     first = 0
     for count in (half - half // 2, half // 2):

time: 103 us -> 101 us (0.981)
  Pallas kernels: 73 us -> 70.8 us
    pallas_call x1, Pallas kernels: 4.08 us -> 1.91 us  [cut_for_other(): pl.pallas_call(give_kernel, out_shape=jax.ShapeDtypeStruct((sources, coun...]
  transfers between devices with their start and end apart: 5 -> 5, of which waited for: 2 -> 2; matrix products, arithmetic and copies ran while one was open for 4% -> 4% of each run, Pallas kernels for 49% -> 50%
where the time goes in v4:
time: 101 us
  Pallas kernels  70.8 us (70%)
  starting transfers between devices  11.1 us (11%)
  other arithmetic  8.44 us (8%)
  local copies, waits for them, and re-layouts  5.2 us (5%)
  waiting for transfers between devices  4.9 us (5%)
    pallas_call x1, Pallas kernels, make_steering(): pl.pallas_call(steering_kernel, out_shape=jax.ShapeDtypeStruct((count, be...  35.5 us
    pallas_call x2, Pallas kernels, multiply(): pl.pallas_call(functools.partial(product_kernel, scale=1.0 / math.sqrt(ch...  28.8 us
    all_to_all x1, starting transfers between devices, shared_beams(): received = lax.all_to_all(rows, 'chan', 0, 0)  7.26 us
    pallas_call x1, Pallas kernels, spectra_rows(): pl.pallas_call(spectra_kernel, out_shape=jax.ShapeDtypeStruct((bin_count,...  4.61 us
    unnamed x12, local copies, waits for them, and re-layouts  4.18 us
    select_n x1, other arithmetic, shared_beams(): jnp.where(core == 0, jnp.concatenate(kept + swapped), jnp.concatenate(swa...  4.14 us
    ppermute x2, waiting for transfers between devices, shared_beams(): swapped.append(lax.ppermute(other, 'tm', swap))  3.06 us
    another operation x1, other arithmetic  2.56 us
  transfers between devices with their start and end apart: 5, of which 2 were waited for; matrix products, arithmetic and copies ran while one was open for 4% of the time, Pallas kernels for 50%

profile of v4, /device:TPU:0, one launch (start us, length us, event | category | flops | bytes accessed | tf_op | source)
XLA Modules:
  0.0 100.5 jit_solution(11125587982415562632)
XLA Ops:
  0.0 0.0 copy-start.5
  0.0 0.0 copy-start.4
  0.0 0.0 copy-start.3
  0.0 0.9 slice.15
  0.9 1.3 %collective-permute-start = (bf16[128,512]{1,0:T(8,128)(2,1)S(1)}, bf16[128,512]{1,0:T(8,128)(2,1)S(1)}, u32[]{:S(2)}, u32[]{:S(2)}) collective-permute-start(bf16[128,512]{1,0:T(8,128)(2,1)S(1)} %slice.15), channel_id=1, source_target_pairs={{1,0},{2,1},{3,2},{5,4},{6,5},{7,6},{9,8},{10,9},{11,10},{13,12},{... | collective-permute-start | bytes 393224 | tf_op jit(solution)/shard_map/ppermute | solution.py:256
  2.3 2.6 %multiply_convert_fusion.1 = (bf16[96,1024]{1,0:T(8,128)(2,1)S(1)}, bf16[96,1024]{1,0:T(8,128)(2,1)S(1)}) fusion(s32[96]{0:T(128)} %param.7, f32[1024]{0:T(1024)S(1)} %get-tuple-element.23, f32[1024]{0:T(1024)S(1)} %get-tuple-element.24), kind=kLoop, calls=%fused_computation.10 | loop fusion | flops 1966080 | bytes 401792 | tf_op jit(solution)/shard_map/convert
  4.9 0.0 collective-permute-done.next_ref
  4.9 0.0 copy-start.2
  4.9 1.9 %copy-done.2 = bf16[128,12288]{1,0:T(8,128)(2,1)S(1)} copy-done((bf16[128,12288]{1,0:T(8,128)(2,1)S(1)}, bf16[128,12288]{1,0:T(8,128)(2,1)}, u32[]{:S(2)}) %copy-start.2) | copy-done | bytes 3145752
  6.8 4.6 %shard_map.46 = bf16[96,48,128]{2,1,0:T(8,128)(2,1)} custom-call(bf16[192,1024]{1,0:T(8,128)(2,1)S(1)} %pad_maximum_fusion.table_ref, bf16[128,12288]{1,0:T(8,128)(2,1)S(1)} %copy-done.2, bf16[128,512]{1,0:T(8,128)(2,1)S(1)} %collective-permute-done.next_ref), custom_call_target="tpu_custom_call" | custom-call | tf_op jit(solution)/shard_map/pallas_call | solution.py:66
  11.4 7.3 %all-to-all-start = ((bf16[8,12,48,128]{3,2,1,0:T(8,128)(2,1)}), bf16[8,12,48,128]{3,2,1,0:T(8,128)(2,1)S(1)}, u32[]{:S(2)}, u32[]{:S(2)}) async-start(bf16[8,12,48,128]{3,2,1,0:T(8,128)(2,1)} %bitcast.1), calls=%async_computation | async-start | bytes 2359296 | tf_op jit(solution)/shard_map/all_to_all | solution.py:233
  18.7 0.0 copy-done.5
  18.7 0.1 dynamic_slice.7.bins_ref
  18.7 0.0 copy-done.3
  18.8 0.0 copy-done.4
  18.8 1.7 %convert_multiply_fusion.offsets_ref = f32[1024,2048]{1,0:T(8,128)S(1)} fusion(s32[2048]{0:T(1024)S(1)} %bitcast.14, s32[1024]{0:T(1024)S(1)} %bitcast.16, s32[2048]{0:T(1024)S(1)} %bitcast.13, s32[1024]{0:T(1024)S(1)} %bitcast.15), kind=kLoop, calls=%fused_computation | loop fusion | flops 10485760 | bytes 8413184 | tf_op jit(solution)/shard_map/mul | solution.py:263
  20.5 35.5 %shard_map.47.steering_ref = bf16[6,4,2,1024,512]{4,3,2,1,0:T(8,128)(2,1)} custom-call(s32[6]{0:T(128)S(1)} %dynamic_slice.7.bins_ref, f32[1024,2048]{1,0:T(8,128)S(1)} %convert_multiply_fusion.offsets_ref), custom_call_target="tpu_custom_call" | custom-call | flops 251658240 | bytes 50331648 | tf_op jit(solution)/shard_map/pallas_call | solution.py:147
  56.0 0.0 all-to-all-done.received_ref.own_ref
  56.0 0.0 copy-start
  56.0 1.0 %copy-done = bf16[8,12,48,128]{3,2,1,0:T(8,128)(2,1)} copy-done((bf16[8,12,48,128]{3,2,1,0:T(8,128)(2,1)}, bf16[8,12,48,128]{3,2,1,0:T(8,128)(2,1)S(1)}, u32[]{:S(2)}) %copy-start) | copy-done | bytes 1179672
  57.0 1.9 %shard_map.48 = bf16[8,6,48,128]{3,2,1,0:T(8,128)(2,1)} custom-call(s32[1]{0:T(128)} %bitcast.6.at_ref, bf16[8,12,48,128]{3,2,1,0:T(8,128)(2,1)} %copy-done, bf16[6,4,2,1024,512]{4,3,2,1,0:T(8,128)(2,1)} %shard_map.47.steering_ref), custom_call_target="tpu_custom_call" | custom-call | tf_op jit(solution)/shard_map/pallas_call | solution.py:213
  58.9 1.9 %collective-permute-start.1 = (bf16[8,6,48,128]{3,2,1,0:T(8,128)(2,1)}, bf16[8,6,48,128]{3,2,1,0:T(8,128)(2,1)S(1)}, u32[]{:S(2)}, u32[]{:S(2)}) collective-permute-start(bf16[8,6,48,128]{3,2,1,0:T(8,128)(2,1)} %shard_map.48), channel_id=1, source_target_pairs={{0,1},{1,0},{2,3},{3,2},{4,5},{5,4},{6,7},{7,6},{8,9},{9,8},{10,11... | collective-permute-start | bytes 1769480 | tf_op jit(solution)/shard_map/ppermute | solution.py:236
  60.9 1.8 %collective-permute-done.1.other_ref = bf16[8,6,48,128]{3,2,1,0:T(8,128)(2,1)S(1)} collective-permute-done((bf16[8,6,48,128]{3,2,1,0:T(8,128)(2,1)}, bf16[8,6,48,128]{3,2,1,0:T(8,128)(2,1)S(1)}, u32[]{:S(2)}, u32[]{:S(2)}) %collective-permute-start.1) | collective-permute-done | bytes 589856 | tf_op jit(solution)/shard_map/ppermute | solution.py:236
  62.7 0.0 copy-start.1
  62.7 1.3 %copy-done.1 = bf16[8,12,48,128]{3,2,1,0:T(8,128)(2,1)S(1)} copy-done((bf16[8,12,48,128]{3,2,1,0:T(8,128)(2,1)S(1)}, bf16[8,12,48,128]{3,2,1,0:T(8,128)(2,1)}, u32[]{:S(2)}) %copy-start.1) | copy-done | bytes 1179672
  64.0 14.0 %shard_map.49 = (f32[3,48,2048]{2,1,0:T(8,128)S(1)}, f32[3,48,2048]{2,1,0:T(8,128)S(1)}) custom-call(s32[1]{0:T(128)} %bitcast.at_ref, bf16[6,4,2,1024,512]{4,3,2,1,0:T(8,128)(2,1)} %shard_map.47.steering_ref, bf16[8,12,48,128]{3,2,1,0:T(8,128)(2,1)S(1)} %copy-done.1, bf16[8,6,48,128]{3,2,1,0:T(8,128)(2,1)S(1)} %collective-permute-done.1.other_ref), custom_call_target="tpu_custom_call" | custom-call | flops 2415919104 | bytes 27525120 | tf_op jit(solution)/shard_map/pallas_call | solution.py:184
  78.0 0.4 collective-permute-start.2
  78.5 14.7 %shard_map.50 = (f32[3,48,2048]{2,1,0:T(8,128)S(1)}, f32[3,48,2048]{2,1,0:T(8,128)}) custom-call(s32[1]{0:T(128)} %bitcast.at_ref, bf16[6,4,2,1024,512]{4,3,2,1,0:T(8,128)(2,1)} %shard_map.47.steering_ref, bf16[8,12,48,128]{3,2,1,0:T(8,128)(2,1)S(1)} %copy-done.1, bf16[8,6,48,128]{3,2,1,0:T(8,128)(2,1)S(1)} %collective-permute-done.1.other_ref), custom_call_target="tpu_custom_call" | custom-call | flops 2415919104 | bytes 27525120 | tf_op jit(solution)/shard_map/pallas_call | solution.py:184
  93.2 0.1 collective-permute-start.3
  93.3 0.0 collective-permute-done.2
  93.3 3.1 %collective-permute-done.3 = f32[3,48,2048]{2,1,0:T(8,128)} collective-permute-done((f32[3,48,2048]{2,1,0:T(8,128)}, f32[3,48,2048]{2,1,0:T(8,128)}, u32[]{:S(2)}, u32[]{:S(2)}) %collective-permute-start.3) | collective-permute-done | bytes 1179680 | tf_op jit(solution)/shard_map/ppermute | solution.py:244
  96.4 4.1 %maximum_select_fusion = f32[12,2,24,2048]{3,2,1,0:T(8,128)} fusion(f32[3,2,24,2048]{3,2,1,0:T(8,128)} %bitcast.10, f32[3,2,24,2048]{3,2,1,0:T(8,128)} %bitcast.9, f32[3,2,24,2048]{3,2,1,0:T(8,128)S(1)} %bitcast.12, f32[3,2,24,2048]{3,2,1,0:T(8,128)S(1)} %bitcast.11, pred[]{:T(512)S(6)} %eq.5), kind=kLoop, calls=%fused_computation.1 | loop fusion | flops 8257536 | bytes 9437185 | tf_op jit(solution)/shard_map/jit(_where)/select_n | solution.py:246
  (4 shorter events, 0.1 us)
Async XLA Ops:
  0.0 18.7 %copy-start.5 = (s32[96]{0:T(128)S(1)}, s32[96]{0:T(128)}, u32[]{:S(2)}) copy-start(s32[96]{0:T(128)} %param.7) | copy-start | bytes 1156
  0.0 18.8 %copy-start.4 = (s32[2,1024]{1,0:T(2,128)S(1)}, s32[2,1024]{1,0:T(2,128)}, u32[]{:S(2)}) copy-start(s32[2,1024]{1,0:T(2,128)} %param.5) | copy-start | bytes 24580
  0.0 18.7 %copy-start.3 = (s32[2,2048]{1,0:T(2,128)S(1)}, s32[2,2048]{1,0:T(2,128)}, u32[]{:S(2)}) copy-start(s32[2,2048]{1,0:T(2,128)} %param.6) | copy-start | bytes 49156
  0.9 3.9 %collective-permute-start = (bf16[128,512]{1,0:T(8,128)(2,1)S(1)}, bf16[128,512]{1,0:T(8,128)(2,1)S(1)}, u32[]{:S(2)}, u32[]{:S(2)}) collective-permute-start(bf16[128,512]{1,0:T(8,128)(2,1)S(1)} %slice.15), channel_id=1, source_target_pairs={{1,0},{2,1},{3,2},{5,4},{6,5},{7,6},{9,8},{10,9},{11,10},{13,12},{... | collective-permute-start | bytes 393224 | tf_op jit(solution)/shard_map/ppermute | solution.py:256
  4.9 1.9 %copy-start.2 = (bf16[128,12288]{1,0:T(8,128)(2,1)S(1)}, bf16[128,12288]{1,0:T(8,128)(2,1)}, u32[]{:S(2)}) copy-start(bf16[128,12288]{1,0:T(8,128)(2,1)} %wave_ref.1) | copy-start | bytes 9437188
  11.4 44.6 %all-to-all-start = ((bf16[8,12,48,128]{3,2,1,0:T(8,128)(2,1)}), bf16[8,12,48,128]{3,2,1,0:T(8,128)(2,1)S(1)}, u32[]{:S(2)}, u32[]{:S(2)}) async-start(bf16[8,12,48,128]{3,2,1,0:T(8,128)(2,1)} %bitcast.1), calls=%async_computation | async-start | bytes 2359296 | tf_op jit(solution)/shard_map/all_to_all | solution.py:233
  56.0 1.0 %copy-start = (bf16[8,12,48,128]{3,2,1,0:T(8,128)(2,1)}, bf16[8,12,48,128]{3,2,1,0:T(8,128)(2,1)S(1)}, u32[]{:S(2)}) copy-start(bf16[8,12,48,128]{3,2,1,0:T(8,128)(2,1)S(1)} %all-to-all-done.received_ref.own_ref) | copy-start | bytes 3538948
  58.9 3.8 %collective-permute-start.1 = (bf16[8,6,48,128]{3,2,1,0:T(8,128)(2,1)}, bf16[8,6,48,128]{3,2,1,0:T(8,128)(2,1)S(1)}, u32[]{:S(2)}, u32[]{:S(2)}) collective-permute-start(bf16[8,6,48,128]{3,2,1,0:T(8,128)(2,1)} %shard_map.48), channel_id=1, source_target_pairs={{0,1},{1,0},{2,3},{3,2},{4,5},{5,4},{6,7},{7,6},{8,9},{9,8},{10,11... | collective-permute-start | bytes 1769480 | tf_op jit(solution)/shard_map/ppermute | solution.py:236
  62.7 1.3 %copy-start.1 = (bf16[8,12,48,128]{3,2,1,0:T(8,128)(2,1)S(1)}, bf16[8,12,48,128]{3,2,1,0:T(8,128)(2,1)}, u32[]{:S(2)}) copy-start(bf16[8,12,48,128]{3,2,1,0:T(8,128)(2,1)} %copy-done) | copy-start | bytes 3538948
  78.0 15.3 %collective-permute-start.2 = (f32[3,48,2048]{2,1,0:T(8,128)S(1)}, f32[3,48,2048]{2,1,0:T(8,128)}, u32[]{:S(2)}, u32[]{:S(2)}) collective-permute-start(f32[3,48,2048]{2,1,0:T(8,128)S(1)} %get-tuple-element.15), channel_id=1, source_target_pairs={{0,1},{1,0},{2,3},{3,2},{4,5},{5,4},{6,7},{7,6},{8,9},{9,8},{10,11... | collective-permute-start | bytes 3538952 | tf_op jit(solution)/shard_map/ppermute | solution.py:244
  93.2 3.2 %collective-permute-start.3 = (f32[3,48,2048]{2,1,0:T(8,128)}, f32[3,48,2048]{2,1,0:T(8,128)}, u32[]{:S(2)}, u32[]{:S(2)}) collective-permute-start(f32[3,48,2048]{2,1,0:T(8,128)} %get-tuple-element.16), channel_id=1, source_target_pairs={{0,1},{1,0},{2,3},{3,2},{4,5},{5,4},{6,7},{7,6},{8,9},{9,8},{10,11... | collective-permute-start | bytes 3538952 | tf_op jit(solution)/shard_map/ppermute | solution.py:244

commit v5 on v4

--- a/solution.py
+++ b/solution.py
@@ -188,7 +188,7 @@
             num_scalar_prefetch=1,
             grid=(count, beams // tile),
             in_specs=[
-                pl.BlockSpec((1, 1, 2, channels, tile), lambda f, j, s: (first + f, j, 0, 0, 0)),
+                pl.BlockSpec((1, 1, 2, channels, tile), lambda f, j, s: (f, j, 0, 0, 0)),
                 pl.BlockSpec(block, lambda f, j, s: (0, s[0] + first + f, 0, 0)),
                 pl.BlockSpec(block, lambda f, j, s: (0, first + f, 0, 0)),
             ],
@@ -232,14 +232,15 @@
     half = own_bins.shape[0] // 2
     received = lax.all_to_all(rows, "chan", 0, 0)
     some_bins = lax.dynamic_slice_in_dim(own_bins, core * half, half, 0)
-    steering = make_steering(some_bins, offsets)
-    partner = lax.ppermute(cut_for_other(1 - core, half, received, steering), "tm", swap)
+    counts = [count for count in (half - 1, 1) if count]
+    steering = [
+        make_steering(some_bins[k * counts[0] : k * counts[0] + count], offsets) for k, count in enumerate(counts)
+    ]
+    partner = lax.ppermute(cut_for_other(1 - core, half, received, steering[0]), "tm", swap)
     kept, swapped = [], []
     first = 0
-    for count in (half - half // 2, half // 2):
-        if count == 0:
-            continue
-        own, other = multiply(core * half, first, count, steering, received, partner)
+    for count, part in zip(counts, steering):
+        own, other = multiply(core * half, first, count, part, received, partner)
         kept.append(own)
         swapped.append(lax.ppermute(other, "tm", swap))
         first += count

time: 101 us -> 109 us (1.079)
  local copies, waits for them, and re-layouts: 5.2 us -> 15.9 us
  waiting for transfers between devices: 4.9 us -> 3.43 us
    unnamed x12 -> x24, local copies, waits for them, and re-layouts: 4.18 us -> 14.2 us
    pallas_call x2, Pallas kernels: 28.8 us -> 26.3 us  [multiply(): pl.pallas_call(functools.partial(product_kernel, scale=1.0 / math.sqrt(ch...]
    ppermute x2, waiting for transfers between devices: 3.06 us -> 1.59 us  [shared_beams(): swapped.append(lax.ppermute(other, 'tm', swap))]
    pallas_call x1 -> x2, Pallas kernels: 35.5 us -> 36.9 us  [make_steering(): pl.pallas_call(steering_kernel, out_shape=jax.ShapeDtypeStruct((count, be...]
  transfers between devices with their start and end apart: 5 -> 5, of which waited for: 2 -> 2; matrix products, arithmetic and copies ran while one was open for 4% -> 5% of each run, Pallas kernels for 50% -> 36%
where the time goes in v5:
time: 109 us
  Pallas kernels  69.8 us (64%)
  local copies, waits for them, and re-layouts  15.9 us (15%)
  starting transfers between devices  11.1 us (10%)
  other arithmetic  8.34 us (8%)
  waiting for transfers between devices  3.43 us (3%)
    pallas_call x2, Pallas kernels, make_steering(): pl.pallas_call(steering_kernel, out_shape=jax.ShapeDtypeStruct((count, be...  36.9 us
    pallas_call x2, Pallas kernels, multiply(): pl.pallas_call(functools.partial(product_kernel, scale=1.0 / math.sqrt(ch...  26.3 us
    unnamed x24, local copies, waits for them, and re-layouts  14.2 us
    all_to_all x1, starting transfers between devices, shared_beams(): received = lax.all_to_all(rows, 'chan', 0, 0)  7.26 us
    pallas_call x1, Pallas kernels, spectra_rows(): pl.pallas_call(spectra_kernel, out_shape=jax.ShapeDtypeStruct((bin_count,...  4.61 us
    select_n x1, other arithmetic, shared_beams(): jnp.where(core == 0, jnp.concatenate(kept + swapped), jnp.concatenate(swa...  4.04 us
    another operation x1, other arithmetic  2.56 us
  transfers between devices with their start and end apart: 5, of which 2 were waited for; matrix products, arithmetic and copies ran while one was open for 5% of the time, Pallas kernels for 36%

profile of v5, /device:TPU:0, one launch (start us, length us, event | category | flops | bytes accessed | tf_op | source)
XLA Modules:
  0.0 108.6 jit_solution(10996361222303057535)
XLA Ops:
  0.0 0.9 slice.22
  0.9 1.3 %collective-permute-start = (bf16[128,512]{1,0:T(8,128)(2,1)S(1)}, bf16[128,512]{1,0:T(8,128)(2,1)S(1)}, u32[]{:S(2)}, u32[]{:S(2)}) collective-permute-start(bf16[128,512]{1,0:T(8,128)(2,1)S(1)} %slice.22), channel_id=1, source_target_pairs={{1,0},{2,1},{3,2},{5,4},{6,5},{7,6},{9,8},{10,9},{11,10},{13,12},{... | collective-permute-start | bytes 393224 | tf_op jit(solution)/shard_map/ppermute | solution.py:257
  2.3 2.6 %multiply_convert_fusion.1 = (bf16[96,1024]{1,0:T(8,128)(2,1)S(1)}, bf16[96,1024]{1,0:T(8,128)(2,1)S(1)}) fusion(s32[96]{0:T(128)} %param.7, f32[1024]{0:T(1024)S(1)} %get-tuple-element.23, f32[1024]{0:T(1024)S(1)} %get-tuple-element.24), kind=kLoop, calls=%fused_computation.10 | loop fusion | flops 1966080 | bytes 401792 | tf_op jit(solution)/shard_map/convert
  4.9 0.0 collective-permute-done.next_ref
  4.9 0.0 copy-start.6
  4.9 1.9 %copy-done.6 = bf16[128,12288]{1,0:T(8,128)(2,1)S(1)} copy-done((bf16[128,12288]{1,0:T(8,128)(2,1)S(1)}, bf16[128,12288]{1,0:T(8,128)(2,1)}, u32[]{:S(2)}) %copy-start.6) | copy-done | bytes 3145752
  6.8 4.6 %shard_map.46 = bf16[96,48,128]{2,1,0:T(8,128)(2,1)} custom-call(bf16[192,1024]{1,0:T(8,128)(2,1)S(1)} %pad_maximum_fusion.table_ref, bf16[128,12288]{1,0:T(8,128)(2,1)S(1)} %copy-done.6, bf16[128,512]{1,0:T(8,128)(2,1)S(1)} %collective-permute-done.next_ref), custom_call_target="tpu_custom_call" | custom-call | tf_op jit(solution)/shard_map/pallas_call | solution.py:66
  11.4 7.3 %all-to-all-start = ((bf16[8,12,48,128]{3,2,1,0:T(8,128)(2,1)}), bf16[8,12,48,128]{3,2,1,0:T(8,128)(2,1)S(1)}, u32[]{:S(2)}, u32[]{:S(2)}) async-start(bf16[8,12,48,128]{3,2,1,0:T(8,128)(2,1)} %bitcast.1), calls=%async_computation | async-start | bytes 2359296 | tf_op jit(solution)/shard_map/all_to_all | solution.py:233
  18.7 0.1 dynamic_slice.7
  18.7 0.0 copy-done.7
  18.8 1.7 %convert_multiply_fusion.offsets_ref = f32[1024,2048]{1,0:T(8,128)S(1)} fusion(s32[2048]{0:T(1024)S(1)} %bitcast.19, s32[1024]{0:T(1024)S(1)} %bitcast.21, s32[2048]{0:T(1024)S(1)} %bitcast.18, s32[1024]{0:T(1024)S(1)} %bitcast.20), kind=kLoop, calls=%fused_computation | loop fusion | flops 10485760 | bytes 8413184 | tf_op jit(solution)/shard_map/mul | solution.py:264
  20.5 30.0 %shard_map.47.steering_ref = bf16[5,4,2,1024,512]{4,3,2,1,0:T(8,128)(2,1)} custom-call(s32[5]{0:T(128)S(1)} %bitcast.16, f32[1024,2048]{1,0:T(8,128)S(1)} %convert_multiply_fusion.offsets_ref), custom_call_target="tpu_custom_call" | custom-call | flops 209715200 | bytes 41943040 | tf_op jit(solution)/shard_map/pallas_call | solution.py:147
  50.5 3.2 %copy-done = f32[1024,2048]{1,0:T(8,128)} copy-done((f32[1024,2048]{1,0:T(8,128)}, f32[1024,2048]{1,0:T(8,128)S(1)}, u32[]{:S(2)}) %copy-start) | copy-done | bytes 8388632
  53.7 0.0 all-to-all-done.received_ref.own_ref
  53.7 1.0 copy-done.3
  54.8 1.9 %shard_map.48 = bf16[8,6,48,128]{3,2,1,0:T(8,128)(2,1)} custom-call(s32[1]{0:T(128)} %bitcast.6.at_ref, bf16[8,12,48,128]{3,2,1,0:T(8,128)(2,1)} %copy-done.3, bf16[5,4,2,1024,512]{4,3,2,1,0:T(8,128)(2,1)} %shard_map.47.steering_ref), custom_call_target="tpu_custom_call" | custom-call | tf_op jit(solution)/shard_map/pallas_call | solution.py:213
  56.7 1.9 %collective-permute-start.1 = (bf16[8,6,48,128]{3,2,1,0:T(8,128)(2,1)}, bf16[8,6,48,128]{3,2,1,0:T(8,128)(2,1)S(1)}, u32[]{:S(2)}, u32[]{:S(2)}) collective-permute-start(bf16[8,6,48,128]{3,2,1,0:T(8,128)(2,1)} %shard_map.48), channel_id=1, source_target_pairs={{0,1},{1,0},{2,3},{3,2},{4,5},{5,4},{6,7},{7,6},{8,9},{9,8},{10,11... | collective-permute-start | bytes 1769480 | tf_op jit(solution)/shard_map/ppermute | solution.py:239
  58.6 1.8 %collective-permute-done.1.other_ref = bf16[8,6,48,128]{3,2,1,0:T(8,128)(2,1)S(1)} collective-permute-done((bf16[8,6,48,128]{3,2,1,0:T(8,128)(2,1)}, bf16[8,6,48,128]{3,2,1,0:T(8,128)(2,1)S(1)}, u32[]{:S(2)}, u32[]{:S(2)}) %collective-permute-start.1) | collective-permute-done | bytes 589856 | tf_op jit(solution)/shard_map/ppermute | solution.py:239
  60.5 1.4 %copy-done.4 = bf16[8,12,48,128]{3,2,1,0:T(8,128)(2,1)S(1)} copy-done((bf16[8,12,48,128]{3,2,1,0:T(8,128)(2,1)S(1)}, bf16[8,12,48,128]{3,2,1,0:T(8,128)(2,1)}, u32[]{:S(2)}) %copy-start.4) | copy-done | bytes 1179672
  61.9 24.3 %shard_map.49 = (f32[5,48,2048]{2,1,0:T(8,128)S(1)}, f32[5,48,2048]{2,1,0:T(8,128)}) custom-call(s32[1]{0:T(128)} %bitcast.at_ref, bf16[5,4,2,1024,512]{4,3,2,1,0:T(8,128)(2,1)} %shard_map.47.steering_ref, bf16[8,12,48,128]{3,2,1,0:T(8,128)(2,1)S(1)} %copy-done.4, bf16[8,6,48,128]{3,2,1,0:T(8,128)(2,1)S(1)} %collective-permute-done.1.other_ref), custom_call_target="tpu_custom_call" | custom-call | flops 4026531840 | bytes 45875200 | tf_op jit(solution)/shard_map/pallas_call | solution.py:184
  86.2 0.4 collective-permute-start.2
  86.6 0.7 slice.27.bins_ref
  87.3 0.0 slice-done.1
  87.3 6.8 %shard_map.50.steering_ref = bf16[1,4,2,1024,512]{4,3,2,1,0:T(8,128)(2,1)S(1)} custom-call(s32[1]{0:T(128)} %slice.27.bins_ref, f32[1024,2048]{1,0:T(8,128)S(1)} %bitcast.13), custom_call_target="tpu_custom_call" | custom-call | flops 41943040 | bytes 8388608 | tf_op jit(solution)/shard_map/pallas_call | solution.py:147
  94.1 0.0 copy-start.1
  94.1 3.3 %copy-done.1 = bf16[1,4,2,1024,512]{4,3,2,1,0:T(8,128)(2,1)} copy-done((bf16[1,4,2,1024,512]{4,3,2,1,0:T(8,128)(2,1)}, bf16[1,4,2,1024,512]{4,3,2,1,0:T(8,128)(2,1)S(1)}, u32[]{:S(2)}) %copy-start.1) | copy-done | bytes 8388632
  97.4 3.4 %copy-done.2 = bf16[1,4,2,1024,512]{4,3,2,1,0:T(8,128)(2,1)S(1)} copy-done((bf16[1,4,2,1024,512]{4,3,2,1,0:T(8,128)(2,1)S(1)}, bf16[1,4,2,1024,512]{4,3,2,1,0:T(8,128)(2,1)}, u32[]{:S(2)}) %copy-start.2) | copy-done | bytes 8388632
  100.8 2.0 %shard_map.51 = (f32[1,48,2048]{2,1,0:T(8,128)S(1)}, f32[1,48,2048]{2,1,0:T(8,128)S(1)}) custom-call(s32[1]{0:T(128)} %bitcast.at_ref, bf16[1,4,2,1024,512]{4,3,2,1,0:T(8,128)(2,1)S(1)} %copy-done.2, bf16[8,12,48,128]{3,2,1,0:T(8,128)(2,1)S(1)} %copy-done.5, bf16[8,6,48,128]{3,2,1,0:T(8,128)(2,1)S(1)} %collective-permute-done.1.other_ref), custom_call_target="tpu_custom_call" | custom-call | flops 805306368 | bytes 9175040 | tf_op jit(solution)/shard_map/pallas_call | solution.py:184
  102.8 0.2 collective-permute-start.3
  103.0 1.6 %collective-permute-done.3 = f32[1,48,2048]{2,1,0:T(8,128)S(1)} collective-permute-done((f32[1,48,2048]{2,1,0:T(8,128)S(1)}, f32[1,48,2048]{2,1,0:T(8,128)S(1)}, u32[]{:S(2)}, u32[]{:S(2)}) %collective-permute-start.3) | collective-permute-done | bytes 393248 | tf_op jit(solution)/shard_map/ppermute | solution.py:245
  104.6 0.0 collective-permute-done.2
  104.6 4.0 %maximum_select_fusion = f32[12,2,24,2048]{3,2,1,0:T(8,128)} fusion(f32[1,2,24,2048]{3,2,1,0:T(8,128)S(1)} %bitcast.17, f32[5,2,24,2048]{3,2,1,0:T(8,128)} %bitcast.9, f32[1,2,24,2048]{3,2,1,0:T(8,128)S(1)} %bitcast.15, f32[5,2,24,2048]{3,2,1,0:T(8,128)S(1)} %bitcast.14, pred[]{:T(512)S(6)} %eq.5), kind=kLoop, calls=%fused_computation.1 | loop fusion | flops 8257536 | bytes 9437185 | tf_op jit(solution)/shard_map/jit(_where)/select_n | solution.py:247
  (19 shorter events, 0.1 us)
Async XLA Ops:
  0.0 18.7 %copy-start.9 = (s32[96]{0:T(128)S(1)}, s32[96]{0:T(128)}, u32[]{:S(2)}) copy-start(s32[96]{0:T(128)} %param.7) | copy-start | bytes 1156
  0.0 18.8 %copy-start.8 = (s32[2,1024]{1,0:T(2,128)S(1)}, s32[2,1024]{1,0:T(2,128)}, u32[]{:S(2)}) copy-start(s32[2,1024]{1,0:T(2,128)} %param.5) | copy-start | bytes 24580
  0.0 18.7 %copy-start.7 = (s32[2,2048]{1,0:T(2,128)S(1)}, s32[2,2048]{1,0:T(2,128)}, u32[]{:S(2)}) copy-start(s32[2,2048]{1,0:T(2,128)} %param.6) | copy-start | bytes 49156
  0.9 3.9 %collective-permute-start = (bf16[128,512]{1,0:T(8,128)(2,1)S(1)}, bf16[128,512]{1,0:T(8,128)(2,1)S(1)}, u32[]{:S(2)}, u32[]{:S(2)}) collective-permute-start(bf16[128,512]{1,0:T(8,128)(2,1)S(1)} %slice.22), channel_id=1, source_target_pairs={{1,0},{2,1},{3,2},{5,4},{6,5},{7,6},{9,8},{10,9},{11,10},{13,12},{... | collective-permute-start | bytes 393224 | tf_op jit(solution)/shard_map/ppermute | solution.py:257
  4.9 1.9 %copy-start.6 = (bf16[128,12288]{1,0:T(8,128)(2,1)S(1)}, bf16[128,12288]{1,0:T(8,128)(2,1)}, u32[]{:S(2)}) copy-start(bf16[128,12288]{1,0:T(8,128)(2,1)} %wave_ref.1) | copy-start | bytes 9437188
  11.4 42.3 %all-to-all-start = ((bf16[8,12,48,128]{3,2,1,0:T(8,128)(2,1)}), bf16[8,12,48,128]{3,2,1,0:T(8,128)(2,1)S(1)}, u32[]{:S(2)}, u32[]{:S(2)}) async-start(bf16[8,12,48,128]{3,2,1,0:T(8,128)(2,1)} %bitcast.1), calls=%async_computation | async-start | bytes 2359296 | tf_op jit(solution)/shard_map/all_to_all | solution.py:233
  50.5 3.2 %copy-start = (f32[1024,2048]{1,0:T(8,128)}, f32[1024,2048]{1,0:T(8,128)S(1)}, u32[]{:S(2)}) copy-start(f32[1024,2048]{1,0:T(8,128)S(1)} %convert_multiply_fusion.offsets_ref) | copy-start | bytes 25165828
  53.7 1.0 copy-start.3
  56.7 3.8 %collective-permute-start.1 = (bf16[8,6,48,128]{3,2,1,0:T(8,128)(2,1)}, bf16[8,6,48,128]{3,2,1,0:T(8,128)(2,1)S(1)}, u32[]{:S(2)}, u32[]{:S(2)}) collective-permute-start(bf16[8,6,48,128]{3,2,1,0:T(8,128)(2,1)} %shard_map.48), channel_id=1, source_target_pairs={{0,1},{1,0},{2,3},{3,2},{4,5},{5,4},{6,7},{7,6},{8,9},{9,8},{10,11... | collective-permute-start | bytes 1769480 | tf_op jit(solution)/shard_map/ppermute | solution.py:239
  60.5 26.8 %slice-start = ((s8[8388608]{0:T(1024)(128)(4,1)}), s8[4194304]{0:T(1024)(128)(4,1)S(1)}, s32[]{:S(2)}) async-start(s8[8388608]{0:T(1024)(128)(4,1)} %bitcast.12), calls=%async_computation.1 | async-start | bytes 8388608
  60.5 1.4 %copy-start.4 = (bf16[8,12,48,128]{3,2,1,0:T(8,128)(2,1)S(1)}, bf16[8,12,48,128]{3,2,1,0:T(8,128)(2,1)}, u32[]{:S(2)}) copy-start(bf16[8,12,48,128]{3,2,1,0:T(8,128)(2,1)} %copy-done.3) | copy-start | bytes 3538948
  61.9 25.4 %slice-start.1 = ((s8[8388608]{0:T(1024)(128)(4,1)}), s8[4194304]{0:T(1024)(128)(4,1)S(1)}, s32[]{:S(2)}) async-start(s8[8388608]{0:T(1024)(128)(4,1)} %bitcast.12), calls=%async_computation.2 | async-start | bytes 8388608
  86.2 18.4 %collective-permute-start.2 = (f32[5,48,2048]{2,1,0:T(8,128)}, f32[5,48,2048]{2,1,0:T(8,128)}, u32[]{:S(2)}, u32[]{:S(2)}) collective-permute-start(f32[5,48,2048]{2,1,0:T(8,128)} %get-tuple-element.15), channel_id=1, source_target_pairs={{0,1},{1,0},{2,3},{3,2},{4,5},{5,4},{6,7},{7,6},{8,9},{9,8},{10,11... | collective-permute-start | bytes 5898248 | tf_op jit(solution)/shard_map/ppermute | solution.py:245
  87.3 10.1 %copy-start.5 = (bf16[8,12,48,128]{3,2,1,0:T(8,128)(2,1)S(1)}, bf16[8,12,48,128]{3,2,1,0:T(8,128)(2,1)}, u32[]{:S(2)}) copy-start(bf16[8,12,48,128]{3,2,1,0:T(8,128)(2,1)} %copy-done.3) | copy-start | bytes 3538948
  94.1 3.3 %copy-start.1 = (bf16[1,4,2,1024,512]{4,3,2,1,0:T(8,128)(2,1)}, bf16[1,4,2,1024,512]{4,3,2,1,0:T(8,128)(2,1)S(1)}, u32[]{:S(2)}) copy-start(bf16[1,4,2,1024,512]{4,3,2,1,0:T(8,128)(2,1)S(1)} %shard_map.50.steering_ref) | copy-start | bytes 25165828
  97.4 3.4 %copy-start.2 = (bf16[1,4,2,1024,512]{4,3,2,1,0:T(8,128)(2,1)S(1)}, bf16[1,4,2,1024,512]{4,3,2,1,0:T(8,128)(2,1)}, u32[]{:S(2)}) copy-start(bf16[1,4,2,1024,512]{4,3,2,1,0:T(8,128)(2,1)} %copy-done.1) | copy-start | bytes 25165828
  102.8 1.8 %collective-permute-start.3 = (f32[1,48,2048]{2,1,0:T(8,128)S(1)}, f32[1,48,2048]{2,1,0:T(8,128)S(1)}, u32[]{:S(2)}, u32[]{:S(2)}) collective-permute-start(f32[1,48,2048]{2,1,0:T(8,128)S(1)} %get-tuple-element.16), channel_id=1, source_target_pairs={{0,1},{1,0},{2,3},{3,2},{4,5},{5,4},{6,7},{7,6},{8,9},{9,8},{10,11... | collective-permute-start | bytes 1179656 | tf_op jit(solution)/shard_map/ppermute | solution.py:245
